TPU v7x, 512 devices: a whole 4x4x16 slice. The times are simulated.
512 devices in a mesh: seq: 64 (over z, x), head: 8 (over y, core).
Axes of the slice: x: 4, y: 4, z: 16, core: 2. Of those that a mesh axis runs over, the one named last changes fastest.
Arguments:
- hidden_in: bfloat16 [8192, 2048], P(('seq', 'head')), may hold values from -6 to 6
- w_inner: bfloat16 [2048, 4096], P(None, 'head'), may hold values from -0.125 to 0.125
- w_inout: bfloat16 [2048, 512], replicated, may hold values from -0.00390625 to 0.00390625
- w_step: bfloat16 [2, 2048, 64], P(None, None, 'head'), may hold values from -0.125 to 0.125
- step_bias: float32 [2, 64], P(None, 'head'), may hold values from -1 to 1
- decay_rate: float32 [64], P('head'), may hold values from 2e-05 to 0.05
- skip_gain: float32 [64], P('head'), may hold values from 0.5 to 1.5
Outputs:
- mixed: bfloat16 [8192, 4096], P('seq', 'head')
All inputs are finite; a program needn't handle non-finite values.
Results may differ from a plain program's by a relative error of at most 0.0052.
Values may be sent and summed in bfloat16 or wider, within the bound.
No kernel may reach another device: no remote copies, remote signals or barrier semaphores. Data moves between devices by JAX's collectives and lax.ppermute only.
A program may use at most 128 MiB of HBM per device.

v0:
```python
import jax
import jax.numpy as jnp
from jax import lax
from jax.sharding import PartitionSpec as P

HEADDIM = 64
SPAN = 128


def carried_in(part, axis, combine, identity, reverse):
    count = lax.axis_size(axis)
    place = lax.axis_index(axis)
    ahead = count - 1 - place if reverse else place
    gathered = jax.tree.map(lambda a: lax.all_gather(a, axis), part)
    state = jax.tree.map(lambda a, e: jnp.zeros_like(a) + jnp.asarray(e, a.dtype), part, identity)

    def one(lap, state):
        source = count - 1 - lap if reverse else lap
        return combine(
            state, jax.tree.map(lambda a: lax.dynamic_index_in_dim(a, source, 0, False), gathered)
        )

    return lax.fori_loop(0, ahead, one, state)


def span_pass(inner, in_map, out_map, steps, rate):
    rows, heads_here, width = inner.shape
    count = rows // SPAN
    states = in_map.shape[1]
    exact = lax.Precision.HIGHEST
    values = inner.astype(jnp.float32).reshape(count, SPAN, heads_here, width)
    in_blocks = in_map.astype(jnp.float32).reshape(count, SPAN, states)
    out_blocks = out_map.astype(jnp.float32).reshape(count, SPAN, states)
    logs = (-steps * rate[None, :]).reshape(count, SPAN, heads_here).transpose(0, 2, 1)
    step_blocks = steps.reshape(count, SPAN, heads_here).transpose(0, 2, 1)
    cums = jnp.cumsum(logs, axis=2)
    scores = jnp.einsum("kin,kjn->kij", out_blocks, in_blocks, precision=exact)
    spread = cums[:, :, :, None] - cums[:, :, None, :]
    lower = jnp.arange(SPAN)[:, None] > jnp.arange(SPAN)[None, :]
    decay = jnp.where(lower, jnp.exp(jnp.where(lower, spread, 0.0)), 0.0)
    weights = decay * scores[:, None, :, :] * step_blocks[:, :, None, :]
    intra = jnp.einsum("khij,kjhp->kihp", weights, values, precision=exact)
    tail = jnp.exp(cums[:, :, -1:] - cums) * step_blocks
    pieces = jnp.einsum("khj,kjn,kjhp->khnp", tail, in_blocks, values, precision=exact)
    totals = cums[:, :, -1]

    def advance(carry, item):
        total, piece = item
        return (jnp.exp(total)[:, None, None] * carry + piece, carry)

    last, starts = lax.scan(
        advance, jnp.zeros((heads_here, states, width), jnp.float32), (totals, pieces)
    )
    inter = jnp.einsum("khi,kin,khnp->kihp", jnp.exp(cums), out_blocks, starts, precision=exact)
    before = jnp.cumsum(totals, axis=0) - totals
    reach = cums + before[:, :, None]
    local = (intra + inter).reshape(rows, heads_here, width)
    return (local, last, jnp.exp(jnp.sum(totals, axis=0)), reach)


def incoming(reach, out_map, state, shape):
    count = reach.shape[0]
    out_blocks = out_map.astype(jnp.float32).reshape(count, SPAN, out_map.shape[1])
    added = jnp.einsum(
        "khi,kin,hnp->kihp", jnp.exp(reach), out_blocks, state, precision=lax.Precision.HIGHEST
    )
    return added.reshape(shape)


def combine(earlier, later):
    return (earlier[0] * later[0], later[0][:, None, None] * earlier[1] + later[1])


def shards(hidden_in, w_inner, w_inout, w_step, step_bias, decay_rate, skip_gain):
    heads_here = w_step.shape[2]
    width = w_inner.shape[1]
    states = w_inout.shape[1] // 4
    piece = lax.all_gather(hidden_in, "head", axis=0, tiled=True)
    first = jnp.dot(piece, w_inner, preferred_element_type=jnp.float32)
    second = jnp.dot(piece, w_inout, preferred_element_type=jnp.float32)
    third = jnp.dot(piece, w_step[0], preferred_element_type=jnp.float32)
    fourth = jnp.dot(piece, w_step[1], preferred_element_type=jnp.float32)
    joined = jnp.concatenate([first, second, third, fourth], axis=1)
    rows = joined.shape[0]
    inner = joined[:, :width].astype(jnp.bfloat16).reshape(rows, heads_here, HEADDIM)
    maps = joined[:, width : width + 4 * states].astype(jnp.bfloat16)
    offset = width + 4 * states
    step_fwd = jax.nn.softplus(joined[:, offset : offset + heads_here] + step_bias[0][None, :])
    step_bwd = jax.nn.softplus(
        joined[:, offset + heads_here : offset + 2 * heads_here] + step_bias[1][None, :]
    )
    in_fwd = maps[:, :states]
    out_fwd = maps[:, states : 2 * states]
    in_bwd = jnp.flip(maps[:, 2 * states : 3 * states], 0)
    out_bwd = jnp.flip(maps[:, 3 * states :], 0)
    local_fwd, state_fwd, decay_fwd, reach_fwd = span_pass(
        inner, in_fwd, out_fwd, step_fwd, decay_rate
    )
    local_bwd, state_bwd, decay_bwd, reach_bwd = span_pass(
        jnp.flip(inner, 0), in_bwd, out_bwd, jnp.flip(step_bwd, 0), decay_rate
    )
    identity = (jnp.ones((heads_here,), jnp.float32), jnp.zeros_like(state_fwd))
    before_fwd = carried_in((decay_fwd, state_fwd), "seq", combine, identity, False)
    before_bwd = carried_in((decay_bwd, state_bwd), "seq", combine, identity, True)
    ahead = local_fwd + incoming(reach_fwd, out_fwd, before_fwd[1], local_fwd.shape)
    behind = local_bwd + incoming(reach_bwd, out_bwd, before_bwd[1], local_bwd.shape)
    mixed = ahead + jnp.flip(behind, 0) + skip_gain[None, :, None] * inner.astype(jnp.float32)
    return mixed.reshape(rows, width).astype(jnp.bfloat16)


def solution(mesh):
    placed = (
        P(("seq", "head"), None),
        P(None, "head"),
        P(),
        P(None, None, "head"),
        P(None, "head"),
        P("head"),
        P("head"),
    )
    return jax.shard_map(
        shards, mesh=mesh, in_specs=placed, out_specs=P("seq", "head"), check_vma=False
    )
```

profile of v0, /device:TPU:486, one launch (start us, length us, event | category | flops | bytes accessed | tf_op | source)
XLA Modules:
  0.0 549.0 jit_solution(18041093198861668920)
XLA Ops:
  6.5 14.0 %all_gather.19 = bf16[128,2048]{1,0:T(8,128)(2,1)S(1)} all-gather(bf16[16,2048]{1,0:T(8,128)(2,1)} %param.11), channel_id=1, replica_groups=mesh['seq'=64,'head'=8] {'head'}, dimensions={0}, use_global_device_ids=true | all-gather | bytes 589824 | tf_op jit(solution)/shard_map/all_gather | solution.py:78
  21.3 1.0 compare_select_fusion
  22.3 1.0 compare_select_fusion.1
  25.2 2.1 convolution_convert_fusion.1
  27.5 1.0 fusion.7
  30.3 73.6 %all-gather.1 = f32[64,8,1]{1,2,0:T(1,128)} all-gather(f32[1,8,1]{1,2,0:T(1,128)S(1)} %copy.38), channel_id=3, replica_groups=mesh['seq'=64,'head'=8] {'seq'}, dimensions={0}, use_global_device_ids=true | all-gather | bytes 2080 | tf_op jit(solution)/shard_map/all_gather | solution.py:14
  104.0 76.8 %all-gather = f32[64,8,1]{1,2,0:T(1,128)} all-gather(f32[1,8,1]{1,2,0:T(1,128)S(1)} %copy.32), channel_id=2, replica_groups=mesh['seq'=64,'head'=8] {'seq'}, dimensions={0}, use_global_device_ids=true | all-gather | bytes 2080 | tf_op jit(solution)/shard_map/all_gather | solution.py:14
  185.3 1.0 fusion.52
  186.3 30.4 %all-gather.7.cloned.1.call-done = f32[64,8,128,64]{2,3,1,0:T(8,128)} async-done(((f32[1,8,128,64]{2,3,1,0:T(8,128)}), f32[64,8,128,64]{2,3,1,0:T(8,128)}) %all-gather.7.cloned.1.call-update) | async-done | bytes 16777232 | tf_op jit(solution)/shard_map/all_gather | solution.py:14
  216.9 1.0 fusion.66
  217.9 1.8 fusion.11
  220.5 188.7 %all-gather.5.cloned.1.call-done = f32[64,8,128,64]{2,3,1,0:T(8,128)} async-done(((f32[1,8,128,64]{2,3,1,0:T(8,128)}), f32[64,8,128,64]{2,3,1,0:T(8,128)}) %all-gather.5.cloned.1.call-update) | async-done | bytes 16777232 | tf_op jit(solution)/shard_map/all_gather | solution.py:14
  409.3 129.0 %while.16 = (s32[]{:T(128)}, f32[8,128,64]{2,1,0:T(8,128)S(1)}, s32[]{:T(128)}, f32[64,8]{1,0:T(8,128)}, f32[64,8,128,64]{2,3,1,0:T(8,128)}, /*index=5*/s32[]{:T(128)}, s32[]{:T(128)}, s32[]{:T(128)}) while((s32[]{:T(128)}, f32[8,128,64]{2,1,0:T(8,128)S(1)}, s32[]{:T(128)}, f32[64,8]{1,0:T(8,128)}, f32[64,8,128,64]{2,3,1,0:T(8,128)}, ...), condition=%wide.region_2.3_spmd, body=%wide.region_1.2_spmd.sunk | while | flops 131077 | bytes 1835231 | solution.py:23
  409.3 1.0 constant_dynamic-slice_fusion.4
  411.4 1.0 constant_dynamic-slice_fusion.4
  413.4 1.0 constant_dynamic-slice_fusion.4
  417.5 1.0 constant_dynamic-slice_fusion.4
  421.6 1.0 constant_dynamic-slice_fusion.4
  425.7 1.0 constant_dynamic-slice_fusion.4
  427.7 1.0 constant_dynamic-slice_fusion.4
  433.8 1.0 constant_dynamic-slice_fusion.4
  435.9 1.0 constant_dynamic-slice_fusion.4
  437.9 1.0 constant_dynamic-slice_fusion.4
  460.5 1.0 constant_dynamic-slice_fusion.4
  464.6 1.0 constant_dynamic-slice_fusion.4
  466.6 1.0 constant_dynamic-slice_fusion.4
  470.7 1.0 constant_dynamic-slice_fusion.4
  472.8 1.0 constant_dynamic-slice_fusion.4
  476.9 1.0 constant_dynamic-slice_fusion.4
  483.0 1.0 constant_dynamic-slice_fusion.4
  538.5 1.0 fusion.50
  539.5 1.8 fusion.12
  (283 shorter events, 121.1 us)
Async XLA Ops:
  6.5 18.1 %copy-start = (bf16[2048,512]{1,0:T(8,128)(2,1)S(1)}, bf16[2048,512]{1,0:T(8,128)(2,1)}, u32[]{:S(2)}) copy-start(bf16[2048,512]{1,0:T(8,128)(2,1)} %param.13) | copy-start | bytes 6291460
  6.5 210.1 %all-gather.7.cloned.1.call-start = ((), (), s32[]{:S(2)}) async-start(), calls=%async_computation.1 | async-start | bytes 17039360 | tf_op jit(solution)/shard_map/all_gather | solution.py:14
  25.1 160.1 %copy-start.1 = (bf16[128,512]{1,0:T(8,128)(2,1)}, bf16[128,512]{1,0:T(8,128)(2,1)S(1)}, u32[]{:S(2)}) copy-start(bf16[128,512]{1,0:T(8,128)(2,1)S(1)} %convolution_convert_fusion) | copy-start | bytes 393220
  27.5 2.7 copy-start.3
  28.5 380.7 %all-gather.5.cloned.1.call-start = ((), (), s32[]{:S(2)}) async-start(), calls=%async_computation | async-start | bytes 17039360 | tf_op jit(solution)/shard_map/all_gather | solution.py:14
  30.2 186.4 %copy-start.2 = (bf16[128,128]{1,0:T(8,128)(2,1)}, bf16[128,128]{1,0:T(8,128)(2,1)S(1)}, u32[]{:S(2)}) copy-start(bf16[128,128]{1,0:T(8,128)(2,1)S(1)} %rev.21) | copy-start | bytes 98308
  409.3 130.2 %copy-start.4 = (f32[128,8]{0,1:T(8,128)S(1)}, f32[128,8]{0,1:T(8,128)}, u32[]{:S(2)}) copy-start(f32[128,8]{0,1:T(8,128)} %get-tuple-element.221) | copy-start | bytes 12292
Sparse Core Ops, SparseCore 0:
  28.6 187.9 all-gather.6
  219.6 189.5 all-gather.4
where the time goes:
time: 553 us; the launch traced here: 549 us
  waiting for transfers between devices  219 us (40%)
  blocking collectives  164 us (30%)
  local copies, waits for them, and re-layouts  121 us (22%)
  matrix products  15.7 us (3%)
  between operations  13.6 us (2%)
  other arithmetic  12.9 us (2%)
    all_gather x2, waiting for transfers between devices, carried_in(): gathered = jax.tree.map(lambda a: lax.all_gather(a, axis), part)  219 us
    all_gather x2, blocking collectives, carried_in(): gathered = jax.tree.map(lambda a: lax.all_gather(a, axis), part)  150 us
    dynamic_slice x126, local copies, waits for them, and re-layouts, one(): lax.dynamic_index_in_dim(a, source, 0, False)  73.9 us
    mul x63, local copies, waits for them, and re-layouts, combine(): later[0][:, None, None] * earlier[1] + later[1]  43.4 us
    all_gather x1, blocking collectives, shards(): piece = lax.all_gather(hidden_in, 'head', axis=0, tiled=True)  14 us
  transfers between devices with their start and end apart: 2, of which 2 were waited for; matrix products, arithmetic and copies ran while one was open for 2% of the time, Pallas kernels for 0%

commit v1 on v0

v1 whole, which is shorter than its diff:
```python
import jax
import jax.numpy as jnp
from jax import lax
from jax.experimental import pallas as pl
from jax.experimental.pallas import tpu as pltpu
from jax.sharding import PartitionSpec as P

SPAN = 128
HEADDIM = 64
STATE = 128
EXTRA = 8
F32 = jnp.float32
BF16 = jnp.bfloat16
LAST = (((1,), (1,)), ((), ()))
FIRST = (((0,), (0,)), ((), ()))


def dot(a, b, dims=None, precision=None):
    dims = dims or (((1,), (0,)), ((), ()))
    return lax.dot_general(a, b, dims, precision=precision, preferred_element_type=F32)


def iota(shape, dim):
    return lax.broadcasted_iota(jnp.int32, shape, dim)


def local_kernel(x_ref, wi_ref, wm_ref, ws_ref, bias_ref, rate_ref, gain_ref, send_ref, y_ref, out_ref, reach_ref):
    owners = send_ref.shape[0]
    heads = rate_ref.shape[1] // 2
    share = heads * HEADDIM // owners
    x = x_ref[...]
    pre = dot(x, ws_ref[...], LAST) + bias_ref[...]
    step = jnp.maximum(pre, 0.0) + jnp.log1p(jnp.exp(-jnp.abs(pre)))
    logs = -rate_ref[...] * step
    row, col = iota((SPAN, SPAN), 0), iota((SPAN, SPAN), 1)
    lower, upper = row > col, row < col
    exact = lax.Precision.HIGHEST
    ahead = dot((row >= col).astype(F32), logs, precision=exact)
    behind = dot((row <= col).astype(F32), logs, precision=exact)
    forward = iota(logs.shape, 1) < heads
    cum = jnp.where(forward, ahead, behind)
    total = jnp.where(forward[:1], cum[SPAN - 1 :], cum[:1])
    tail = jnp.exp(total - cum) * step
    reach_ref[...] = jnp.exp(cum)
    decay = jnp.exp(total)
    cum_t, step_t = cum.T, step.T

    maps = dot(x, wm_ref[...]).astype(BF16)
    in_f, out_f = maps[:, :STATE], maps[:, STATE : 2 * STATE]
    in_b, out_b = maps[:, 2 * STATE : 3 * STATE], maps[:, 3 * STATE :]
    out_ref[:, :STATE] = out_f
    out_ref[:, STATE:] = out_b
    scores = jnp.where(lower, dot(out_f, in_f, LAST), jnp.where(upper, dot(out_b, in_b, LAST), 0.0))
    in_f32, in_b32 = in_f.astype(F32), in_b.astype(F32)
    inner = dot(x, wi_ref[...]).astype(BF16)
    mark = iota((EXTRA, STATE), 0)
    left = iota((SPAN, 2 * HEADDIM), 1) < HEADDIM
    zero = jnp.zeros((SPAN, 2 * HEADDIM), BF16)

    for pair in range(heads // 2):
        both = inner[:, 2 * HEADDIM * pair : 2 * HEADDIM * (pair + 1)]
        weights = []
        for h in (2 * pair, 2 * pair + 1):
            g = h + heads
            spread = jnp.where(
                lower,
                cum[:, h : h + 1] - cum_t[h : h + 1],
                cum[:, g : g + 1] - cum_t[g : g + 1],
            )
            steps = jnp.where(lower, step_t[h : h + 1], step_t[g : g + 1])
            weights.append((jnp.exp(spread) * (scores * steps)).astype(BF16))
            tailed = jnp.concatenate([in_f32 * tail[:, h : h + 1], in_b32 * tail[:, g : g + 1]], axis=1).astype(BF16)
            piece = dot(both[:, HEADDIM * (h % 2) : HEADDIM * (h % 2 + 1)], tailed, FIRST)
            piece = piece.reshape(HEADDIM // share, share, 2 * STATE)
            first = h * (HEADDIM // share)
            chunks = pl.ds(first, HEADDIM // share)
            rows = jnp.concatenate([piece[:, :, :STATE], piece[:, :, STATE:]], axis=1)
            send_ref[chunks, 0 : 2 * share, :] = rows.astype(BF16)
            d_f, d_b = decay[:, h : h + 1], decay[:, g : g + 1]
            high_f, high_b = d_f.astype(BF16).astype(F32), d_b.astype(BF16).astype(F32)
            marks = jnp.where(mark == 0, high_f, 0.0) + jnp.where(mark == 1, d_f - high_f, 0.0)
            marks = marks + jnp.where(mark == 2, high_b, 0.0) + jnp.where(mark == 3, d_b - high_b, 0.0)
            send_ref[chunks, 2 * share : 2 * share + EXTRA, :] = jnp.broadcast_to(
                marks[None], (HEADDIM // share, EXTRA, STATE)
            ).astype(BF16)
        stacked = jnp.concatenate([jnp.where(left, both, zero), jnp.where(left, zero, both)], axis=0)
        here = slice(2 * HEADDIM * pair, 2 * HEADDIM * (pair + 1))
        y_ref[:, here] = dot(jnp.concatenate(weights, axis=1), stacked) + gain_ref[:, here] * both.astype(F32)


def scan_kernel(got_ref, back_ref, held):
    blocks = got_ref.shape[0]
    share = back_ref.shape[1] // 2
    zero = jnp.zeros((share, STATE), F32)

    def one(step, carry):
        state_f, state_b = carry
        other = blocks - 1 - step
        held[step, :share] = state_f
        held[other, share:] = state_b
        here, there = got_ref[step].astype(F32), got_ref[other].astype(F32)
        d_f = here[2 * share : 2 * share + 1] + here[2 * share + 1 : 2 * share + 2]
        d_b = there[2 * share + 2 : 2 * share + 3] + there[2 * share + 3 : 2 * share + 4]
        return d_f * state_f + here[:share], d_b * state_b + there[share : 2 * share]

    lax.fori_loop(0, blocks, one, (zero, zero), unroll=4)
    back_ref[...] = held[...].astype(BF16)


def final_kernel(state_ref, out_ref, reach_ref, y_ref, mixed_ref):
    owners, rows, _ = state_ref.shape
    share = rows // 2
    heads = reach_ref.shape[1] // 2
    state = state_ref[...].astype(F32)
    ahead = state[:, :share].reshape(owners * share, STATE).astype(BF16)
    behind = state[:, share:].reshape(owners * share, STATE).astype(BF16)
    far_f = dot(out_ref[:, :STATE], ahead, LAST)
    far_b = dot(out_ref[:, STATE:], behind, LAST)
    reach = reach_ref[...]
    left = iota((SPAN, 2 * HEADDIM), 1) < HEADDIM
    for pair in range(heads // 2):
        here = slice(2 * HEADDIM * pair, 2 * HEADDIM * (pair + 1))
        h, g = 2 * pair, 2 * pair + heads
        scale_f = jnp.where(left, reach[:, h : h + 1], reach[:, h + 1 : h + 2])
        scale_b = jnp.where(left, reach[:, g : g + 1], reach[:, g + 1 : g + 2])
        mixed_ref[:, here] = (y_ref[:, here] + scale_f * far_f[:, here] + scale_b * far_b[:, here]).astype(BF16)


def call(kernel, out_shape, flops, scratch=()):
    return pl.pallas_call(
        kernel,
        out_shape=out_shape,
        scratch_shapes=list(scratch),
        compiler_params=pltpu.CompilerParams(vmem_limit_bytes=24 * 1024 * 1024),
        cost_estimate=pl.CostEstimate(flops=flops, bytes_accessed=1 << 20, transcendentals=0),
    )


def shards(hidden_in, w_inner, w_inout, w_step, step_bias, decay_rate, skip_gain):
    heads = w_step.shape[2]
    width = w_inner.shape[1]
    blocks = lax.axis_size("seq")
    share = width // blocks
    rows = 2 * share
    x = lax.all_gather(hidden_in, "head", axis=0, tiled=True)
    w_rows = w_step.transpose(0, 2, 1).reshape(2 * heads, -1)
    bias = step_bias.reshape(1, 2 * heads)
    rate = jnp.concatenate([decay_rate, decay_rate])[None, :]
    gain = jnp.repeat(skip_gain, HEADDIM)[None, :]
    shape = jax.ShapeDtypeStruct
    send, near, outs, reach = call(
        local_kernel,
        (
            shape((blocks, rows + EXTRA, STATE), BF16),
            shape((SPAN, width), F32),
            shape((SPAN, 2 * STATE), BF16),
            shape((SPAN, 2 * heads), F32),
        ),
        700_000_000,
    )(x, w_inner, w_inout, w_rows, bias, rate, gain)
    got = lax.all_to_all(send, "seq", 0, 0, tiled=True)
    back = call(
        scan_kernel,
        shape((blocks, rows, STATE), BF16),
        1_000_000,
        (pltpu.VMEM((blocks, rows, STATE), F32),),
    )(got)
    state = lax.all_to_all(back, "seq", 0, 0, tiled=True)
    return call(final_kernel, shape((SPAN, width), BF16), 40_000_000)(state, outs, reach, near)


def solution(mesh):
    placed = (
        P(("seq", "head"), None),
        P(None, "head"),
        P(),
        P(None, None, "head"),
        P(None, "head"),
        P("head"),
        P("head"),
    )
    return jax.shard_map(
        shards, mesh=mesh, in_specs=placed, out_specs=P("seq", "head"), check_vma=False
    )
```

time: 553 us -> 97.2 us (0.18)
  the two profiles are of different devices: /device:TPU:486 before, /device:TPU:8 now
where the time goes in v1:
time: 97.2 us; the launch traced here: 96.9 us
  blocking collectives  87.2 us (90%)
  local copies, waits for them, and re-layouts  5.58 us (6%)
  Pallas kernels  3.26 us (3%)
    all_to_all x1, blocking collectives, shards(): got = lax.all_to_all(send, 'seq', 0, 0, tiled=True)  43.5 us
    all_to_all x1, blocking collectives, shards(): state = lax.all_to_all(back, 'seq', 0, 0, tiled=True)  27.6 us
    all_gather x1, blocking collectives, shards(): x = lax.all_gather(hidden_in, 'head', axis=0, tiled=True)  16.1 us
    unnamed x6, local copies, waits for them, and re-layouts  4.02 us

profile of v1, /device:TPU:8, one launch (start us, length us, event | category | flops | bytes accessed | tf_op | source)
XLA Modules:
  0.0 96.9 jit_solution(10574183712506082816)
XLA Ops:
  0.0 0.8 reshape.7.bias_ref
  0.8 0.8 maximum_bitcast_fusion.rate_ref
  1.6 0.7 broadcast_in_dim.7
  2.3 0.1 broadcast_in_dim_reshape.3.gain_ref
  2.4 16.1 %all_gather.3.x_ref = bf16[128,2048]{1,0:T(8,128)(2,1)S(1)} all-gather(bf16[16,2048]{1,0:T(8,128)(2,1)} %param.7), channel_id=1, replica_groups=mesh['seq'=64,'head'=8] {'head'}, dimensions={0}, use_global_device_ids=true | all-gather | bytes 589824 | tf_op jit(solution)/shard_map/all_gather | solution.py:145
  18.4 0.0 copy-start
  18.4 1.6 %copy-done = bf16[2048,512]{1,0:T(8,128)(2,1)S(1)} copy-done((bf16[2048,512]{1,0:T(8,128)(2,1)S(1)}, bf16[2048,512]{1,0:T(8,128)(2,1)}, u32[]{:S(2)}) %copy-start) | copy-done | bytes 2097176
  20.0 0.0 copy-start.1
  20.0 1.6 %copy-done.1 = bf16[2048,512]{1,0:T(8,128)(2,1)S(1)} copy-done((bf16[2048,512]{1,0:T(8,128)(2,1)S(1)}, bf16[2048,512]{1,0:T(8,128)(2,1)}, u32[]{:S(2)}) %copy-start.1) | copy-done | bytes 2097176
  21.6 0.0 copy-start.2
  21.6 0.8 copy-done.2
  22.5 1.9 %shard_map.73 = (bf16[64,24,128]{2,1,0:T(8,128)(2,1)S(1)}, f32[128,512]{1,0:T(8,128)S(1)}, bf16[128,256]{1,0:T(8,128)(2,1)S(1)}, f32[128,16]{1,0:T(8,128)S(1)}) custom-call(bf16[128,2048]{1,0:T(8,128)(2,1)S(1)} %all_gather.3.x_ref, bf16[2048,512]{1,0:T(8,128)(2,1)S(1)} %copy-done, bf16[2048,512]{1,0:T(8,128)(2,1)S(1)} %copy-done.1, ...), custom_call_target="tpu_custom_call" | custom-call | flops 700000000 | bytes 1048576 | tf_op jit(solution)/shard_map/pallas_call | solution.py:151
  24.4 43.5 %all_to_all.10.got_ref = bf16[64,24,128]{2,1,0:T(8,128)(2,1)S(1)} all-to-all(bf16[64,24,128]{2,1,0:T(8,128)(2,1)S(1)} %get-tuple-element.9), channel_id=1, replica_groups=mesh['seq'=64,'head'=8] {'seq'}, dimensions={0} | all-to-all | bytes 786432 | tf_op jit(solution)/shard_map/all_to_all | solution.py:161
  67.9 0.3 shard_map.74
  68.2 27.6 %all_to_all.11.state_ref = bf16[64,16,128]{2,1,0:T(8,128)(2,1)S(1)} all-to-all(bf16[64,16,128]{2,1,0:T(8,128)(2,1)S(1)} %shard_map.74), channel_id=1, replica_groups=mesh['seq'=64,'head'=8] {'seq'}, dimensions={0} | all-to-all | bytes 524288 | tf_op jit(solution)/shard_map/all_to_all | solution.py:168
  95.9 1.0 %shard_map.75 = bf16[128,512]{1,0:T(8,128)(2,1)} custom-call(bf16[64,16,128]{2,1,0:T(8,128)(2,1)S(1)} %all_to_all.11.state_ref, bf16[128,256]{1,0:T(8,128)(2,1)S(1)} %get-tuple-element.10.out_ref, f32[128,16]{1,0:T(8,128)S(1)} %get-tuple-element.11.reach_ref, f32[128,512]{1,0:T(8,128)S(1)} %get-tuple-element.12.y_ref), custom_call_target="tpu_custom_call" | custom-call | flops 40000000 | bytes 1048576 | tf_op jit(solution)/shard_map/pallas_call | solution.py:169
Async XLA Ops:
  18.4 1.6 %copy-start = (bf16[2048,512]{1,0:T(8,128)(2,1)S(1)}, bf16[2048,512]{1,0:T(8,128)(2,1)}, u32[]{:S(2)}) copy-start(bf16[2048,512]{1,0:T(8,128)(2,1)} %wi_ref.1) | copy-start | bytes 6291460
  20.0 1.6 %copy-start.1 = (bf16[2048,512]{1,0:T(8,128)(2,1)S(1)}, bf16[2048,512]{1,0:T(8,128)(2,1)}, u32[]{:S(2)}) copy-start(bf16[2048,512]{1,0:T(8,128)(2,1)} %wm_ref.1) | copy-start | bytes 6291460
  21.6 0.8 copy-start.2

commit v2 on v1

v2 whole, which is shorter than its diff:
```python
import jax
import jax.numpy as jnp
from jax import lax
from jax.experimental import pallas as pl
from jax.experimental.pallas import tpu as pltpu
from jax.sharding import Mesh, PartitionSpec as P

SPAN = 128
HEADDIM = 64
STATE = 128
EXTRA = 8
CUTS = 4
F32 = jnp.float32
BF16 = jnp.bfloat16
LAST = (((1,), (1,)), ((), ()))
FIRST = (((0,), (0,)), ((), ()))
VMEM = pl.BlockSpec(memory_space=pltpu.VMEM)
HBM = pl.BlockSpec(memory_space=pltpu.HBM)


def dot(a, b, dims=None, precision=None):
    dims = dims or (((1,), (0,)), ((), ()))
    return lax.dot_general(a, b, dims, precision=precision, preferred_element_type=F32)


def iota(shape, dim):
    return lax.broadcasted_iota(jnp.int32, shape, dim)


def split(value, first):
    mark = iota((EXTRA, STATE), 0)
    high = value.astype(BF16).astype(F32)
    return jnp.where(mark == first, high, 0.0) + jnp.where(mark == first + 1, value - high, 0.0)


def joined(rows, first):
    return rows[first : first + 1] + rows[first + 1 : first + 2]


def fetch(pairs, sems):
    waits, used = [], 0
    for src, dst in pairs:
        cuts = CUTS if src.shape[0] % (16 * CUTS) == 0 else 1
        size = src.shape[0] // cuts
        copies = []
        for cut in range(cuts):
            part = pl.ds(cut * size, size)
            ends = (src.at[part], dst.at[part]) if cuts > 1 else (src, dst)
            copies.append(pltpu.make_async_copy(*ends, sems.at[used + cut]))
        used += cuts
        for copy in copies:
            copy.start()
        waits.append(copies)
    return waits


def ready(copies):
    for copy in copies:
        copy.wait()


def local_kernel(mine_ref, other_ref, *refs):
    ws_ref, small_ref, *sources = refs[:4]
    send_ref, y_ref, out_ref, reach_ref = refs[4:8]
    wm_ref, wi_ref = held = refs[8:10]
    sems = refs[10]
    waits = fetch(zip(sources, held), sems)
    heads = send_ref.shape[0]
    first = lax.axis_index("core") == 0
    parts = []
    for y in range(mine_ref.shape[0]):
        mine, other = mine_ref[y], other_ref[y]
        parts += [jnp.where(first, mine, other), jnp.where(first, other, mine)]
    x = jnp.concatenate(parts, axis=0)
    bias_f, bias_b, rate, gain = (small_ref[row : row + 1] for row in range(4))
    rate = jnp.concatenate([rate, rate], axis=1)
    pre = dot(x, ws_ref[...].astype(BF16), LAST) + jnp.concatenate([bias_f, bias_b], axis=1)
    step = jnp.maximum(pre, 0.0) + jnp.log1p(jnp.exp(-jnp.abs(pre)))
    logs = -rate * step
    row, col = iota((SPAN, SPAN), 0), iota((SPAN, SPAN), 1)
    lower, upper = row > col, row < col
    exact = lax.Precision.HIGHEST
    ahead = dot((row >= col).astype(F32), logs, precision=exact)
    behind = dot((row <= col).astype(F32), logs, precision=exact)
    forward = iota(logs.shape, 1) < heads
    cum = jnp.where(forward, ahead, behind)
    total = jnp.where(forward[:1], cum[SPAN - 1 :], cum[:1])
    tail = jnp.exp(total - cum) * step
    reach_ref[...] = jnp.exp(cum)
    decay = jnp.exp(total)
    cum_t, step_t = cum.T, step.T

    ready(waits[0])
    maps = dot(x, wm_ref[...]).astype(BF16)
    in_f, out_f = maps[:, :STATE], maps[:, STATE : 2 * STATE]
    in_b, out_b = maps[:, 2 * STATE : 3 * STATE], maps[:, 3 * STATE :]
    out_ref[:, :STATE] = out_f
    out_ref[:, STATE:] = out_b
    scores = jnp.where(lower, dot(out_f, in_f, LAST), jnp.where(upper, dot(out_b, in_b, LAST), 0.0))
    in_f32, in_b32 = in_f.astype(F32), in_b.astype(F32)
    weights, tailed = [], []
    for h in range(heads):
        g = h + heads
        spread = jnp.where(
            lower,
            cum[:, h : h + 1] - cum_t[h : h + 1],
            cum[:, g : g + 1] - cum_t[g : g + 1],
        )
        steps = jnp.where(lower, step_t[h : h + 1], step_t[g : g + 1])
        weights.append((jnp.exp(spread) * (scores * steps)).astype(BF16))
        both = [in_f32 * tail[:, h : h + 1], in_b32 * tail[:, g : g + 1]]
        tailed.append(jnp.concatenate(both, axis=1).astype(BF16))
        marks = split(decay[:, h : h + 1], 0) + split(decay[:, g : g + 1], 2)
        send_ref[h, 2 * HEADDIM :] = marks.astype(BF16)

    ready(waits[1])
    inner = dot(x, wi_ref[...]).astype(BF16)
    left = iota((SPAN, 2 * HEADDIM), 1) < HEADDIM
    zero = jnp.zeros((SPAN, 2 * HEADDIM), BF16)
    for pair in range(heads // 2):
        here = slice(2 * HEADDIM * pair, 2 * HEADDIM * (pair + 1))
        both = inner[:, here]
        for h in (2 * pair, 2 * pair + 1):
            piece = dot(both[:, HEADDIM * (h % 2) : HEADDIM * (h % 2 + 1)], tailed[h], FIRST).astype(BF16)
            send_ref[h, :HEADDIM] = piece[:, :STATE]
            send_ref[h, HEADDIM : 2 * HEADDIM] = piece[:, STATE:]
        stacked = jnp.concatenate([jnp.where(left, both, zero), jnp.where(left, zero, both)], axis=0)
        gains = jnp.where(left, gain[:, 2 * pair : 2 * pair + 1], gain[:, 2 * pair + 1 : 2 * pair + 2])
        mixing = jnp.concatenate(weights[2 * pair : 2 * pair + 2], axis=1)
        y_ref[:, here] = dot(mixing, stacked) + gains * both.astype(F32)


def forward_part(rows):
    rows = rows.astype(F32)
    return joined(rows[2 * HEADDIM :], 0), rows[:HEADDIM]


def backward_part(rows):
    rows = rows.astype(F32)
    return joined(rows[2 * HEADDIM :], 2), rows[HEADDIM : 2 * HEADDIM]


def total_kernel(got_ref, send_ref):
    blocks, groups = got_ref.shape[0], send_ref.shape[0]
    place = lax.axis_index("zgroup")
    decay_f = decay_b = jnp.ones((1, STATE), F32)
    state_f = state_b = jnp.zeros((HEADDIM, STATE), F32)
    for block in range(blocks):
        decay, piece = forward_part(got_ref[block])
        decay_f, state_f = decay * decay_f, decay * state_f + piece
        decay, piece = backward_part(got_ref[blocks - 1 - block])
        decay_b, state_b = decay * decay_b, decay * state_b + piece
    marks_f, marks_b = split(decay_f, 0).astype(BF16), split(decay_b, 0).astype(BF16)
    state_f, state_b = state_f.astype(BF16), state_b.astype(BF16)
    for group in range(groups):
        later = group > place
        send_ref[group, :HEADDIM] = jnp.where(later, state_f, state_b)
        send_ref[group, HEADDIM:] = jnp.where(later, marks_f, marks_b)


def scan_kernel(totals_ref, got_ref, back_ref):
    blocks, groups = got_ref.shape[0], totals_ref.shape[0]
    place = lax.axis_index("zgroup")
    state_f = state_b = jnp.zeros((HEADDIM, STATE), F32)
    for group in range(groups):
        rows = totals_ref[group].astype(F32)
        state_f = jnp.where(group < place, joined(rows[HEADDIM:], 0) * state_f + rows[:HEADDIM], state_f)
        other = groups - 1 - group
        rows = totals_ref[other].astype(F32)
        state_b = jnp.where(other > place, joined(rows[HEADDIM:], 0) * state_b + rows[:HEADDIM], state_b)
    for block in range(blocks):
        back_ref[block, :HEADDIM] = state_f.astype(BF16)
        decay, piece = forward_part(got_ref[block])
        state_f = decay * state_f + piece
        other = blocks - 1 - block
        back_ref[other, HEADDIM:] = state_b.astype(BF16)
        decay, piece = backward_part(got_ref[other])
        state_b = decay * state_b + piece


def final_kernel(state_ref, out_ref, reach_ref, y_ref, mixed_ref):
    heads = state_ref.shape[0]
    ahead = state_ref[:, :HEADDIM].reshape(heads * HEADDIM, STATE)
    behind = state_ref[:, HEADDIM:].reshape(heads * HEADDIM, STATE)
    far_f = dot(out_ref[:, :STATE], ahead, LAST)
    far_b = dot(out_ref[:, STATE:], behind, LAST)
    reach = reach_ref[...]
    left = iota((SPAN, 2 * HEADDIM), 1) < HEADDIM
    for pair in range(heads // 2):
        here = slice(2 * HEADDIM * pair, 2 * HEADDIM * (pair + 1))
        h, g = 2 * pair, 2 * pair + heads
        scale_f = jnp.where(left, reach[:, h : h + 1], reach[:, h + 1 : h + 2])
        scale_b = jnp.where(left, reach[:, g : g + 1], reach[:, g + 1 : g + 2])
        mixed_ref[:, here] = (y_ref[:, here] + scale_f * far_f[:, here] + scale_b * far_b[:, here]).astype(BF16)


def call(kernel, out_shape, flops, **kwargs):
    return pl.pallas_call(
        kernel,
        out_shape=out_shape,
        compiler_params=pltpu.CompilerParams(vmem_limit_bytes=24 * 1024 * 1024),
        cost_estimate=pl.CostEstimate(flops=flops, bytes_accessed=1 << 20, transcendentals=0),
        **kwargs,
    )


def shards(hidden_in, w_inner, w_inout, w_step, step_bias, decay_rate, skip_gain):
    heads = w_step.shape[2]
    width = w_inner.shape[1]
    columns = lax.axis_size("y")
    groups = lax.axis_size("zgroup")
    shape = jax.ShapeDtypeStruct
    copies = jnp.broadcast_to(hidden_in[None], (columns, *hidden_in.shape))
    mine = lax.all_to_all(copies, "y", 0, 0, tiled=True)
    other = lax.ppermute(mine, "core", [(0, 1), (1, 0)])
    small = jnp.concatenate([step_bias, decay_rate[None], skip_gain[None]], axis=0)
    w_rows = w_step.transpose(0, 2, 1).reshape(2 * heads, -1).astype(F32)
    sources = (w_inout, w_inner)
    send, near, outs, reach = pl.pallas_call(
        local_kernel,
        out_shape=(
            shape((heads, 2 * HEADDIM + EXTRA, STATE), BF16),
            shape((SPAN, width), F32),
            shape((SPAN, 2 * STATE), BF16),
            shape((SPAN, 2 * heads), F32),
        ),
        in_specs=[VMEM] * 4 + [HBM] * len(sources),
        out_specs=(VMEM,) * 4,
        scratch_shapes=[pltpu.VMEM(a.shape, a.dtype) for a in sources]
        + [pltpu.SemaphoreType.DMA((CUTS * len(sources),))],
        compiler_params=pltpu.CompilerParams(vmem_limit_bytes=52 * 1024 * 1024),
        cost_estimate=pl.CostEstimate(flops=700_000_000, bytes_accessed=6 << 20, transcendentals=0),
    )(mine, other, w_rows, small, *sources)
    got = lax.all_to_all(send, ("zpair", "x"), 0, 0, tiled=True)
    totals = call(total_kernel, shape((groups, HEADDIM + EXTRA, STATE), BF16), 1_000_000)(got)
    totals = lax.all_to_all(totals, "zgroup", 0, 0, tiled=True)
    back = call(scan_kernel, shape((heads, 2 * HEADDIM, STATE), BF16), 1_000_000)(totals, got)
    state = lax.all_to_all(back, ("zpair", "x"), 0, 0, tiled=True)
    return call(final_kernel, shape((SPAN, width), BF16), 40_000_000)(state, outs, reach, near)


def solution(mesh):
    seq, head = mesh.shape["seq"], mesh.shape["head"]
    names = ("zgroup", "zpair", "x", "y", "core")
    fine = Mesh(mesh.devices.reshape(seq // 8, 2, 4, head // 2, 2), names)
    long, wide = ("zgroup", "zpair", "x"), ("y", "core")
    placed = (
        P((*long, *wide), None),
        P(None, wide),
        P(),
        P(None, None, wide),
        P(None, wide),
        P(wide),
        P(wide),
    )
    return jax.shard_map(
        shards, mesh=fine, in_specs=placed, out_specs=P(long, wide), check_vma=False
    )
```

time: 97.2 us -> 73.2 us (0.75)
  blocking collectives: 87.2 us -> 63.7 us
  local copies, waits for them, and re-layouts: 5.58 us -> 0.86 us
  starting transfers between devices: 0 us -> 1.91 us
  Pallas kernels: 3.26 us -> 4.78 us
    all_gather x1 -> x0, blocking collectives: 16.1 us -> none  [shards(): x = lax.all_gather(hidden_in, 'head', axis=0, tiled=True)]
    all_to_all x2 -> x4, blocking collectives: 71.2 us -> 63.7 us  [the longest x1 29 us: shards(): totals = lax.all_to_all(totals, 'zgroup', 0, 0, tiled=True)]
    unnamed x6 -> x0, local copies, waits for them, and re-layouts: 4.02 us -> none
    ppermute x0 -> x1, starting transfers between devices: none -> 1.91 us  [shards(): other = lax.ppermute(mine, 'core', [(0, 1), (1, 0)])]
    pallas_call x2 -> x3, Pallas kernels: 2.22 us -> 3.75 us  [the longest x1 3.53 us: shards(): pl.pallas_call(local_kernel, out_shape=(shape((heads, 2 * HEADDIM + EXTRA...]
  transfers between devices with their start and end apart: 0 -> 1, of which waited for: 0 -> 0; matrix products, arithmetic and copies ran while one was open for 0% -> 2% of each run, Pallas kernels for 0% -> 0%
where the time goes in v2:
time: 73.2 us; the launch traced here: 72.8 us
  blocking collectives  63.7 us (87%)
  Pallas kernels  4.78 us (7%)
  starting transfers between devices  1.91 us (3%)
  other arithmetic  1.58 us (2%)
  local copies, waits for them, and re-layouts  0.86 us (1%)
    all_to_all x1, blocking collectives, shards(): totals = lax.all_to_all(totals, 'zgroup', 0, 0, tiled=True)  29 us
    all_to_all x1, blocking collectives, shards(): mine = lax.all_to_all(copies, 'y', 0, 0, tiled=True)  13.4 us
    all_to_all x1, blocking collectives, shards(): got = lax.all_to_all(send, ('zpair', 'x'), 0, 0, tiled=True)  11 us
    all_to_all x1, blocking collectives, shards(): state = lax.all_to_all(back, ('zpair', 'x'), 0, 0, tiled=True)  10.2 us
    pallas_call x1, Pallas kernels, shards(): pl.pallas_call(local_kernel, out_shape=(shape((heads, 2 * HEADDIM + EXTRA...  3.53 us
    ppermute x1, starting transfers between devices, shards(): other = lax.ppermute(mine, 'core', [(0, 1), (1, 0)])  1.91 us
  transfers between devices with their start and end apart: 1, of which 0 were waited for; matrix products, arithmetic and copies ran while one was open for 2% of the time, Pallas kernels for 0%

profile of v2, /device:TPU:8, one launch (start us, length us, event | category | flops | bytes accessed | tf_op | source)
XLA Modules:
  0.0 72.8 jit_solution(12344027781099035024)
XLA Ops:
  0.0 0.9 %broadcast_in_dim.12 = bf16[4,16,2048]{2,1,0:T(8,128)(2,1)S(1)} broadcast(bf16[16,2048]{1,0:T(8,128)(2,1)} %param.7), dimensions={1,2} | broadcast | bytes 327680 | tf_op jit(solution)/shard_map/broadcast_in_dim | solution.py:213
  0.9 13.4 %all_to_all.20.mine_ref = bf16[4,16,2048]{2,1,0:T(8,128)(2,1)S(1)} all-to-all(bf16[4,16,2048]{2,1,0:T(8,128)(2,1)S(1)} %broadcast_in_dim.12), channel_id=1, replica_groups=mesh['zgroup'=8,'zpair'=2,'x'=4,'y'=4,'core'=2] {'y'}, dimensions={0} | all-to-all | bytes 524288 | tf_op jit(solution)/shard_map/all_to_all | solution.py:214
  14.3 1.9 %collective-permute-start = (bf16[4,16,2048]{2,1,0:T(8,128)(2,1)S(1)}, bf16[4,16,2048]{2,1,0:T(8,128)(2,1)S(1)}, u32[]{:S(2)}, u32[]{:S(2)}) collective-permute-start(bf16[4,16,2048]{2,1,0:T(8,128)(2,1)S(1)} %all_to_all.20.mine_ref), channel_id=1, source_target_pairs={{0,1},{1,0},{2,3},{3,2},{4,5},{5,4},{6,7},{7,6},{8,9},{9,8},{10,11... | collective-permute-start | bytes 786440 | tf_op jit(solution)/shard_map/ppermute | solution.py:215
  16.2 0.9 %convert_bitcast_fusion.refs_0_ = f32[16,2048]{1,0:T(8,128)S(1)} fusion(bf16[2,2048,8]{1,2,0:T(8,128)(2,1)} %param.10), kind=kLoop, calls=%fused_computation | loop fusion | flops 32768 | bytes 196608 | tf_op jit(solution)/shard_map/convert_element_type | solution.py:217
  17.1 0.7 pad_maximum_fusion.refs_1_
  17.8 0.0 collective-permute-done.other_ref
  17.8 3.5 %shard_map.73 = (bf16[8,136,128]{2,1,0:T(8,128)(2,1)S(1)}, f32[128,512]{1,0:T(8,128)S(1)}, bf16[128,256]{1,0:T(8,128)(2,1)S(1)}, f32[128,16]{1,0:T(8,128)S(1)}) custom-call(bf16[4,16,2048]{2,1,0:T(8,128)(2,1)S(1)} %all_to_all.20.mine_ref, bf16[4,16,2048]{2,1,0:T(8,128)(2,1)S(1)} %collective-permute-done.other_ref, ...), custom_call_target="tpu_custom_call" | custom-call | flops 700000000 | bytes 6291456 | tf_op jit(solution)/shard_map/pallas_call | solution.py:219
  21.3 11.0 %all_to_all.21.got_ref = bf16[8,136,128]{2,1,0:T(8,128)(2,1)S(1)} all-to-all(bf16[8,136,128]{2,1,0:T(8,128)(2,1)S(1)} %get-tuple-element.9), channel_id=1, replica_groups=mesh['zgroup'=8,'zpair'=2,'x'=4,'y'=4,'core'=2] {'zpair','x'}, dimensions={0} | all-to-all | bytes 557056 | tf_op jit(solution)/shard_map/all_to_all | solution.py:234
  32.4 0.1 shard_map.74
  32.5 29.0 %all_to_all.22.totals_ref = bf16[8,72,128]{2,1,0:T(8,128)(2,1)S(1)} all-to-all(bf16[8,72,128]{2,1,0:T(8,128)(2,1)S(1)} %shard_map.74), channel_id=1, replica_groups=mesh['zgroup'=8,'zpair'=2,'x'=4,'y'=4,'core'=2] {'zgroup'}, dimensions={0} | all-to-all | bytes 294912 | tf_op jit(solution)/shard_map/all_to_all | solution.py:236
  61.5 0.1 shard_map.75
  61.6 10.2 %all_to_all.23.state_ref = bf16[8,128,128]{2,1,0:T(8,128)(2,1)S(1)} all-to-all(bf16[8,128,128]{2,1,0:T(8,128)(2,1)S(1)} %shard_map.75), channel_id=1, replica_groups=mesh['zgroup'=8,'zpair'=2,'x'=4,'y'=4,'core'=2] {'zpair','x'}, dimensions={0} | all-to-all | bytes 524288 | tf_op jit(solution)/shard_map/all_to_all | solution.py:238
  71.8 1.0 %shard_map.76 = bf16[128,512]{1,0:T(8,128)(2,1)} custom-call(bf16[8,128,128]{2,1,0:T(8,128)(2,1)S(1)} %all_to_all.23.state_ref, bf16[128,256]{1,0:T(8,128)(2,1)S(1)} %get-tuple-element.10.out_ref, f32[128,16]{1,0:T(8,128)S(1)} %get-tuple-element.11.reach_ref, f32[128,512]{1,0:T(8,128)S(1)} %get-tuple-element.12.y_ref), custom_call_target="tpu_custom_call" | custom-call | flops 40000000 | bytes 1048576 | tf_op jit(solution)/shard_map/pallas_call | solution.py:239
Async XLA Ops:
  14.3 3.5 %collective-permute-start = (bf16[4,16,2048]{2,1,0:T(8,128)(2,1)S(1)}, bf16[4,16,2048]{2,1,0:T(8,128)(2,1)S(1)}, u32[]{:S(2)}, u32[]{:S(2)}) collective-permute-start(bf16[4,16,2048]{2,1,0:T(8,128)(2,1)S(1)} %all_to_all.20.mine_ref), channel_id=1, source_target_pairs={{0,1},{1,0},{2,3},{3,2},{4,5},{5,4},{6,7},{7,6},{8,9},{9,8},{10,11... | collective-permute-start | bytes 786440 | tf_op jit(solution)/shard_map/ppermute | solution.py:215

commit v3 on v2

v3 whole, which is shorter than its diff:
```python
import jax
import jax.numpy as jnp
from jax import lax
from jax.experimental import pallas as pl
from jax.experimental.pallas import tpu as pltpu
from jax.sharding import Mesh, PartitionSpec as P

SPAN = 128
HEADDIM = 64
STATE = 128
EXTRA = 8
CUTS = 1
DEPTH = 2
F32 = jnp.float32
BF16 = jnp.bfloat16
LAST = (((1,), (1,)), ((), ()))
FIRST = (((0,), (0,)), ((), ()))
VMEM = pl.BlockSpec(memory_space=pltpu.VMEM)
HBM = pl.BlockSpec(memory_space=pltpu.HBM)


def dot(a, b, dims=None, precision=None):
    dims = dims or (((1,), (0,)), ((), ()))
    return lax.dot_general(a, b, dims, precision=precision, preferred_element_type=F32)


def iota(shape, dim):
    return lax.broadcasted_iota(jnp.int32, shape, dim)


def split(value, first):
    mark = iota((EXTRA, STATE), 0)
    high = value.astype(BF16).astype(F32)
    return jnp.where(mark == first, high, 0.0) + jnp.where(mark == first + 1, value - high, 0.0)


def joined(rows, first):
    return rows[first : first + 1] + rows[first + 1 : first + 2]


def fetch(pairs, sems):
    waits, used = [], 0
    for src, dst in pairs:
        cuts = CUTS if src.shape[0] % (16 * CUTS) == 0 else 1
        size = src.shape[0] // cuts
        copies = []
        for cut in range(cuts):
            part = pl.ds(cut * size, size)
            ends = (src.at[part], dst.at[part]) if cuts > 1 else (src, dst)
            copies.append(pltpu.make_async_copy(*ends, sems.at[used + cut]))
        used += cuts
        for copy in copies:
            copy.start()
        waits.append(copies)
    return waits


def ready(copies):
    for copy in copies:
        copy.wait()


def local_kernel(x_ref, *refs):
    sources, held, sems = refs[:6], refs[10:16], refs[16]
    send_ref, y_ref, out_ref, reach_ref = refs[6:10]
    ws_ref, bias_ref, rate_ref, gain_ref, wm_ref, wi_ref = held
    waits = fetch(zip(sources, held), sems)
    heads = ws_ref.shape[1]
    share = (send_ref.shape[1] - EXTRA) // 2
    parts = HEADDIM // share
    cores, columns = x_ref.shape[:2]
    x = jnp.concatenate([x_ref[core, y] for y in range(columns) for core in range(cores)], axis=0)
    for copies in waits[:4]:
        ready(copies)
    rate, gain = rate_ref[...].reshape(1, heads), gain_ref[...].reshape(1, heads)
    rate = jnp.concatenate([rate, rate], axis=1)
    pre = [dot(x, ws_ref[side], LAST) + bias_ref[side : side + 1] for side in range(2)]
    pre = jnp.concatenate(pre, axis=1)
    step = jnp.maximum(pre, 0.0) + jnp.log1p(jnp.exp(-jnp.abs(pre)))
    logs = -rate * step
    row, col = iota((SPAN, SPAN), 0), iota((SPAN, SPAN), 1)
    lower, upper = row > col, row < col
    exact = lax.Precision.HIGHEST
    ahead = dot((row >= col).astype(F32), logs, precision=exact)
    behind = dot((row <= col).astype(F32), logs, precision=exact)
    forward = iota(logs.shape, 1) < heads
    cum = jnp.where(forward, ahead, behind)
    total = jnp.where(forward[:1], cum[SPAN - 1 :], cum[:1])
    tail = jnp.exp(total - cum) * step
    reach_ref[...] = jnp.exp(cum)
    decay = jnp.exp(total)
    cum_t, step_t = cum.T, step.T

    ready(waits[4])
    maps = dot(x, wm_ref[...]).astype(BF16)
    in_f, out_f = maps[:, :STATE], maps[:, STATE : 2 * STATE]
    in_b, out_b = maps[:, 2 * STATE : 3 * STATE], maps[:, 3 * STATE :]
    out_ref[:, :STATE] = out_f
    out_ref[:, STATE:] = out_b
    scores = jnp.where(lower, dot(out_f, in_f, LAST), jnp.where(upper, dot(out_b, in_b, LAST), 0.0))
    in_f32, in_b32 = in_f.astype(F32), in_b.astype(F32)
    weights, tailed = [], []
    for h in range(heads):
        g = h + heads
        spread = jnp.where(
            lower,
            cum[:, h : h + 1] - cum_t[h : h + 1],
            cum[:, g : g + 1] - cum_t[g : g + 1],
        )
        steps = jnp.where(lower, step_t[h : h + 1], step_t[g : g + 1])
        weights.append((jnp.exp(spread) * (scores * steps)).astype(BF16))
        both = [in_f32 * tail[:, h : h + 1], in_b32 * tail[:, g : g + 1]]
        tailed.append(jnp.concatenate(both, axis=1).astype(BF16))
        marks = (split(decay[:, h : h + 1], 0) + split(decay[:, g : g + 1], 2)).astype(BF16)
        for part in range(h * parts, (h + 1) * parts):
            send_ref[part, 2 * share :] = marks

    ready(waits[5])
    inner = dot(x, wi_ref[...]).astype(BF16)
    left = iota((SPAN, 2 * HEADDIM), 1) < HEADDIM
    zero = jnp.zeros((SPAN, 2 * HEADDIM), BF16)
    for pair in range(heads // 2):
        here = slice(2 * HEADDIM * pair, 2 * HEADDIM * (pair + 1))
        both = inner[:, here]
        for h in (2 * pair, 2 * pair + 1):
            piece = dot(both[:, HEADDIM * (h % 2) : HEADDIM * (h % 2 + 1)], tailed[h], FIRST).astype(BF16)
            for part in range(parts):
                rows = slice(part * share, (part + 1) * share)
                send_ref[h * parts + part, :share] = piece[rows, :STATE]
                send_ref[h * parts + part, share : 2 * share] = piece[rows, STATE:]
        stacked = jnp.concatenate([jnp.where(left, both, zero), jnp.where(left, zero, both)], axis=0)
        gains = jnp.where(left, gain[:, 2 * pair : 2 * pair + 1], gain[:, 2 * pair + 1 : 2 * pair + 2])
        mixing = jnp.concatenate(weights[2 * pair : 2 * pair + 2], axis=1)
        y_ref[:, here] = dot(mixing, stacked) + gains * both.astype(F32)


def forward_part(rows, share):
    rows = rows.astype(F32)
    return joined(rows[2 * share :], 0), rows[:share]


def backward_part(rows, share):
    rows = rows.astype(F32)
    return joined(rows[2 * share :], 2), rows[share : 2 * share]


def total_kernel(got_ref, send_ref):
    blocks, share = got_ref.shape[0], (got_ref.shape[1] - EXTRA) // 2
    place = lax.axis_index("zgroup")
    decay_f = decay_b = jnp.ones((1, STATE), F32)
    state_f = state_b = jnp.zeros((share, STATE), F32)
    for block in range(blocks):
        decay, piece = forward_part(got_ref[block], share)
        decay_f, state_f = decay * decay_f, decay * state_f + piece
        decay, piece = backward_part(got_ref[blocks - 1 - block], share)
        decay_b, state_b = decay * decay_b, decay * state_b + piece
    marks_f, marks_b = split(decay_f, 0).astype(BF16), split(decay_b, 0).astype(BF16)
    state_f, state_b = state_f.astype(BF16), state_b.astype(BF16)
    for group in range(send_ref.shape[0]):
        later = group > place
        send_ref[group, :share] = jnp.where(later, state_f, state_b)
        send_ref[group, share:] = jnp.where(later, marks_f, marks_b)


def scan_kernel(totals_ref, got_ref, back_ref):
    blocks, share = got_ref.shape[0], back_ref.shape[1] // 2
    groups = totals_ref.shape[0]
    place = lax.axis_index("zgroup")
    state_f = state_b = jnp.zeros((share, STATE), F32)
    for group in range(groups):
        rows = totals_ref[group].astype(F32)
        state_f = jnp.where(group < place, joined(rows[share:], 0) * state_f + rows[:share], state_f)
        other = groups - 1 - group
        rows = totals_ref[other].astype(F32)
        state_b = jnp.where(other > place, joined(rows[share:], 0) * state_b + rows[:share], state_b)
    for block in range(blocks):
        back_ref[block, :share] = state_f.astype(BF16)
        decay, piece = forward_part(got_ref[block], share)
        state_f = decay * state_f + piece
        other = blocks - 1 - block
        back_ref[other, share:] = state_b.astype(BF16)
        decay, piece = backward_part(got_ref[other], share)
        state_b = decay * state_b + piece


def final_kernel(state_ref, out_ref, reach_ref, y_ref, mixed_ref):
    owners, rows, _ = state_ref.shape
    share, heads = rows // 2, reach_ref.shape[1] // 2
    ahead = state_ref[:, :share].reshape(owners * share, STATE)
    behind = state_ref[:, share:].reshape(owners * share, STATE)
    far_f = dot(out_ref[:, :STATE], ahead, LAST)
    far_b = dot(out_ref[:, STATE:], behind, LAST)
    reach = reach_ref[...]
    left = iota((SPAN, 2 * HEADDIM), 1) < HEADDIM
    for pair in range(heads // 2):
        here = slice(2 * HEADDIM * pair, 2 * HEADDIM * (pair + 1))
        h, g = 2 * pair, 2 * pair + heads
        scale_f = jnp.where(left, reach[:, h : h + 1], reach[:, h + 1 : h + 2])
        scale_b = jnp.where(left, reach[:, g : g + 1], reach[:, g + 1 : g + 2])
        mixed_ref[:, here] = (y_ref[:, here] + scale_f * far_f[:, here] + scale_b * far_b[:, here]).astype(BF16)


def call(kernel, out_shape, flops, **kwargs):
    return pl.pallas_call(
        kernel,
        out_shape=out_shape,
        compiler_params=pltpu.CompilerParams(vmem_limit_bytes=24 * 1024 * 1024),
        cost_estimate=pl.CostEstimate(flops=flops, bytes_accessed=1 << 20, transcendentals=0),
        **kwargs,
    )


def shards(hidden_in, w_inner, w_inout, w_step, step_bias, decay_rate, skip_gain):
    heads = w_step.shape[2]
    width = w_inner.shape[1]
    groups = lax.axis_size("zgroup")
    owners = lax.axis_size("zpart") * lax.axis_size("x")
    share = width // owners
    shape = jax.ShapeDtypeStruct
    copies = jnp.broadcast_to(hidden_in[None], (lax.axis_size("y"), *hidden_in.shape))
    x = lax.all_gather(lax.all_to_all(copies, "y", 0, 0, tiled=True), "core", axis=0)
    sources = (w_step.transpose(0, 2, 1), step_bias, decay_rate, skip_gain, w_inout, w_inner)
    sources = tuple(pltpu.with_memory_space_constraint(a, pltpu.HBM) for a in sources)
    send, near, outs, reach = pl.pallas_call(
        local_kernel,
        out_shape=(
            shape((owners, 2 * share + EXTRA, STATE), BF16),
            shape((SPAN, width), F32),
            shape((SPAN, 2 * STATE), BF16),
            shape((SPAN, 2 * heads), F32),
        ),
        in_specs=[VMEM] + [HBM] * len(sources),
        out_specs=(VMEM,) * 4,
        scratch_shapes=[pltpu.VMEM(a.shape, a.dtype) for a in sources]
        + [pltpu.SemaphoreType.DMA((CUTS * len(sources),))],
        compiler_params=pltpu.CompilerParams(vmem_limit_bytes=24 * 1024 * 1024),
        cost_estimate=pl.CostEstimate(flops=700_000_000, bytes_accessed=6 << 20, transcendentals=0),
    )(x, *sources)
    got = lax.all_to_all(send, ("zpart", "x"), 0, 0, tiled=True)
    totals = call(total_kernel, shape((groups, share + EXTRA, STATE), BF16), 1_000_000)(got)
    totals = lax.all_to_all(totals, "zgroup", 0, 0, tiled=True)
    back = call(scan_kernel, shape((owners, 2 * share, STATE), BF16), 1_000_000)(totals, got)
    state = lax.all_to_all(back, ("zpart", "x"), 0, 0, tiled=True)
    return call(final_kernel, shape((SPAN, width), BF16), 40_000_000)(state, outs, reach, near)


def solution(mesh):
    seq, head = mesh.shape["seq"], mesh.shape["head"]
    names = ("zgroup", "zpart", "x", "y", "core")
    fine = Mesh(mesh.devices.reshape(seq // (4 * DEPTH), DEPTH, 4, head // 2, 2), names)
    long, wide = ("zgroup", "zpart", "x"), ("y", "core")
    placed = (
        P((*long, *wide), None),
        P(None, wide),
        P(),
        P(None, None, wide),
        P(None, wide),
        P(wide),
        P(wide),
    )
    return jax.shard_map(
        shards, mesh=fine, in_specs=placed, out_specs=P(long, wide), check_vma=False
    )
```

time: 73.2 us -> 70.8 us (0.967)
  starting transfers between devices: 1.91 us -> 0 us
  other arithmetic: 1.58 us -> 0 us
  blocking collectives: 63.7 us -> 65 us
    all_gather x0 -> x1, blocking collectives: none -> 2.17 us  [shards(): lax.all_gather(lax.all_to_all(copies, 'y', 0, 0, tiled=True), 'core', axi...]
    ppermute x1 -> x0, starting transfers between devices: 1.91 us -> none  [shards(): other = lax.ppermute(mine, 'core', [(0, 1), (1, 0)])]
    convert_element_type x1 -> x0, other arithmetic: 0.85 us -> none  [shards(): w_rows = w_step.transpose(0, 2, 1).reshape(2 * heads, -1).astype(F32)]
  transfers between devices with their start and end apart: 1 -> 0, of which waited for: 0 -> 0; matrix products, arithmetic and copies ran while one was open for 2% -> 0% of each run, Pallas kernels for 0% -> 0%
where the time goes in v3:
time: 70.8 us; the launch traced here: 70.6 us
  blocking collectives  65 us (92%)
  Pallas kernels  4.65 us (7%)
  local copies, waits for them, and re-layouts  0.86 us (1%)
    all_to_all x1, blocking collectives, shards(): totals = lax.all_to_all(totals, 'zgroup', 0, 0, tiled=True)  28.5 us
    all_to_all x1, blocking collectives, shards(): lax.all_to_all(copies, 'y', 0, 0, tiled=True)  13.4 us
    all_to_all x1, blocking collectives, shards(): got = lax.all_to_all(send, ('zpart', 'x'), 0, 0, tiled=True)  10.7 us
    all_to_all x1, blocking collectives, shards(): state = lax.all_to_all(back, ('zpart', 'x'), 0, 0, tiled=True)  10.3 us
    pallas_call x1, Pallas kernels, shards(): pl.pallas_call(local_kernel, out_shape=(shape((owners, 2 * share + EXTRA,...  3.4 us
    all_gather x1, blocking collectives, shards(): lax.all_gather(lax.all_to_all(copies, 'y', 0, 0, tiled=True), 'core', axi...  2.17 us

profile of v3, /device:TPU:8, one launch (start us, length us, event | category | flops | bytes accessed | tf_op | source)
XLA Modules:
  0.0 70.6 jit_solution(13751400250632812739)
XLA Ops:
  0.0 0.9 %broadcast_in_dim.2 = bf16[4,16,2048]{2,1,0:T(8,128)(2,1)S(1)} broadcast(bf16[16,2048]{1,0:T(8,128)(2,1)} %param.7), dimensions={1,2} | broadcast | bytes 327680 | tf_op jit(solution)/shard_map/broadcast_in_dim | solution.py:220
  0.9 13.4 %all_to_all.20 = bf16[4,16,2048]{2,1,0:T(8,128)(2,1)S(1)} all-to-all(bf16[4,16,2048]{2,1,0:T(8,128)(2,1)S(1)} %broadcast_in_dim.2), channel_id=1, replica_groups=mesh['zgroup'=8,'zpart'=2,'x'=4,'y'=4,'core'=2] {'y'}, dimensions={0} | all-to-all | bytes 524288 | tf_op jit(solution)/shard_map/all_to_all | solution.py:221
  14.3 2.2 %all-gather = bf16[8,16,2048]{2,1,0:T(8,128)(2,1)S(1)} all-gather(bf16[4,16,2048]{2,1,0:T(8,128)(2,1)S(1)} %all_to_all.20), channel_id=2, replica_groups=mesh['zgroup'=8,'zpart'=2,'x'=4,'y'=4,'core'=2] {'core'}, dimensions={0}, use_global_device_ids=true | all-gather | bytes 786432 | tf_op jit(solution)/shard_map/all_gather | solution.py:221
  16.5 3.4 %shard_map.73 = (bf16[8,136,128]{2,1,0:T(8,128)(2,1)S(1)}, f32[128,512]{1,0:T(8,128)S(1)}, bf16[128,256]{1,0:T(8,128)(2,1)S(1)}, f32[128,16]{1,0:T(8,128)S(1)}) custom-call(bf16[2,4,16,2048]{3,2,1,0:T(8,128)(2,1)S(1)} %bitcast.2, bf16[2,8,2048]{2,1,0:T(8,128)(2,1)} %bitcast.3, f32[2,8]{1,0:T(2,128)} %refs_1_.1, f32[8]{0:T(128)} %refs_2_.1, f32[8]{0:T(128)} %refs_3_.1, ...), custom_call_target="tpu_custom_call" | custom-call | flops 700000000 | bytes 6291456 | tf_op jit(solution)/shard_map/pallas_call | solution.py:224
  19.9 10.7 %all_to_all.21.got_ref = bf16[8,136,128]{2,1,0:T(8,128)(2,1)S(1)} all-to-all(bf16[8,136,128]{2,1,0:T(8,128)(2,1)S(1)} %get-tuple-element.9), channel_id=1, replica_groups=mesh['zgroup'=8,'zpart'=2,'x'=4,'y'=4,'core'=2] {'zpart','x'}, dimensions={0} | all-to-all | bytes 557056 | tf_op jit(solution)/shard_map/all_to_all | solution.py:239
  30.6 0.1 shard_map.74
  30.7 28.5 %all_to_all.22.totals_ref = bf16[8,72,128]{2,1,0:T(8,128)(2,1)S(1)} all-to-all(bf16[8,72,128]{2,1,0:T(8,128)(2,1)S(1)} %shard_map.74), channel_id=1, replica_groups=mesh['zgroup'=8,'zpart'=2,'x'=4,'y'=4,'core'=2] {'zgroup'}, dimensions={0} | all-to-all | bytes 294912 | tf_op jit(solution)/shard_map/all_to_all | solution.py:241
  59.1 0.1 shard_map.75
  59.3 10.3 %all_to_all.23.state_ref = bf16[8,128,128]{2,1,0:T(8,128)(2,1)S(1)} all-to-all(bf16[8,128,128]{2,1,0:T(8,128)(2,1)S(1)} %shard_map.75), channel_id=1, replica_groups=mesh['zgroup'=8,'zpart'=2,'x'=4,'y'=4,'core'=2] {'zpart','x'}, dimensions={0} | all-to-all | bytes 524288 | tf_op jit(solution)/shard_map/all_to_all | solution.py:243
  69.5 1.0 %shard_map.76 = bf16[128,512]{1,0:T(8,128)(2,1)} custom-call(bf16[8,128,128]{2,1,0:T(8,128)(2,1)S(1)} %all_to_all.23.state_ref, bf16[128,256]{1,0:T(8,128)(2,1)S(1)} %get-tuple-element.10.out_ref, f32[128,16]{1,0:T(8,128)S(1)} %get-tuple-element.11.reach_ref, f32[128,512]{1,0:T(8,128)S(1)} %get-tuple-element.12.y_ref), custom_call_target="tpu_custom_call" | custom-call | flops 40000000 | bytes 1048576 | tf_op jit(solution)/shard_map/pallas_call | solution.py:244

commit v4 on v3

--- a/solution.py
+++ b/solution.py
@@ -11,6 +11,8 @@
 EXTRA = 8
 CUTS = 1
 DEPTH = 2
+Y_ORDER = (0, 2, 1, 3)
+Z_ORDER = (0, 4, 2, 6, 1, 5, 3, 7)
 F32 = jnp.float32
 BF16 = jnp.bfloat16
 LAST = (((1,), (1,)), ((), ()))
@@ -26,6 +28,15 @@
 
 def iota(shape, dim):
     return lax.broadcasted_iota(jnp.int32, shape, dim)
+
+
+def member(place, order):
+    return jnp.where(lax.axis_index("core") == 0, order.index(place), len(order) - 1 - order.index(place))
+
+
+def exchange(array, axis, order):
+    groups = [[2 * place for place in order], [2 * place + 1 for place in reversed(order)]]
+    return lax.all_to_all(array, (axis, "core"), 0, 0, tiled=True, axis_index_groups=groups)
 
 
 def split(value, first):
@@ -68,8 +79,10 @@
     heads = ws_ref.shape[1]
     share = (send_ref.shape[1] - EXTRA) // 2
     parts = HEADDIM // share
-    cores, columns = x_ref.shape[:2]
-    x = jnp.concatenate([x_ref[core, y] for y in range(columns) for core in range(cores)], axis=0)
+    columns = x_ref.shape[1]
+    places = [Y_ORDER.index(y) for y in range(columns)]
+    x = [x_ref[core, columns - 1 - place if core else place] for place in places for core in range(2)]
+    x = jnp.concatenate(x, axis=0)
     for copies in waits[:4]:
         ready(copies)
     rate, gain = rate_ref[...].reshape(1, heads), gain_ref[...].reshape(1, heads)
@@ -157,9 +170,9 @@
     marks_f, marks_b = split(decay_f, 0).astype(BF16), split(decay_b, 0).astype(BF16)
     state_f, state_b = state_f.astype(BF16), state_b.astype(BF16)
     for group in range(send_ref.shape[0]):
-        later = group > place
-        send_ref[group, :share] = jnp.where(later, state_f, state_b)
-        send_ref[group, share:] = jnp.where(later, marks_f, marks_b)
+        later, there = group > place, member(group, Z_ORDER)
+        send_ref[there, :share] = jnp.where(later, state_f, state_b)
+        send_ref[there, share:] = jnp.where(later, marks_f, marks_b)
 
 
 def scan_kernel(totals_ref, got_ref, back_ref):
@@ -168,10 +181,10 @@
     place = lax.axis_index("zgroup")
     state_f = state_b = jnp.zeros((share, STATE), F32)
     for group in range(groups):
-        rows = totals_ref[group].astype(F32)
+        rows = totals_ref[member(group, Z_ORDER)].astype(F32)
         state_f = jnp.where(group < place, joined(rows[share:], 0) * state_f + rows[:share], state_f)
         other = groups - 1 - group
-        rows = totals_ref[other].astype(F32)
+        rows = totals_ref[member(other, Z_ORDER)].astype(F32)
         state_b = jnp.where(other > place, joined(rows[share:], 0) * state_b + rows[:share], state_b)
     for block in range(blocks):
         back_ref[block, :share] = state_f.astype(BF16)
@@ -218,7 +231,7 @@
     share = width // owners
     shape = jax.ShapeDtypeStruct
     copies = jnp.broadcast_to(hidden_in[None], (lax.axis_size("y"), *hidden_in.shape))
-    x = lax.all_gather(lax.all_to_all(copies, "y", 0, 0, tiled=True), "core", axis=0)
+    x = lax.all_gather(exchange(copies, "y", Y_ORDER), "core", axis=0)
     sources = (w_step.transpose(0, 2, 1), step_bias, decay_rate, skip_gain, w_inout, w_inner)
     sources = tuple(pltpu.with_memory_space_constraint(a, pltpu.HBM) for a in sources)
     send, near, outs, reach = pl.pallas_call(
@@ -238,7 +251,7 @@
     )(x, *sources)
     got = lax.all_to_all(send, ("zpart", "x"), 0, 0, tiled=True)
     totals = call(total_kernel, shape((groups, share + EXTRA, STATE), BF16), 1_000_000)(got)
-    totals = lax.all_to_all(totals, "zgroup", 0, 0, tiled=True)
+    totals = exchange(totals, "zgroup", Z_ORDER)
     back = call(scan_kernel, shape((owners, 2 * share, STATE), BF16), 1_000_000)(totals, got)
     state = lax.all_to_all(back, ("zpart", "x"), 0, 0, tiled=True)
     return call(final_kernel, shape((SPAN, width), BF16), 40_000_000)(state, outs, reach, near)

time: 70.8 us -> 68.6 us (0.969)
  blocking collectives: 65 us -> 62.8 us
    all_to_all x2, blocking collectives: 41.9 us -> 39.1 us  [exchange(): lax.all_to_all(array, (axis, 'core'), 0, 0, tiled=True, axis_index_groups...]
where the time goes in v4:
time: 68.6 us; the launch traced here: 68.3 us
  blocking collectives  62.8 us (92%)
  Pallas kernels  4.66 us (7%)
  local copies, waits for them, and re-layouts  0.86 us (1%)
    all_to_all x2, blocking collectives, exchange(): lax.all_to_all(array, (axis, 'core'), 0, 0, tiled=True, axis_index_groups...  39.1 us
    all_to_all x1, blocking collectives, shards(): state = lax.all_to_all(back, ('zpart', 'x'), 0, 0, tiled=True)  10.9 us
    all_to_all x1, blocking collectives, shards(): got = lax.all_to_all(send, ('zpart', 'x'), 0, 0, tiled=True)  10.7 us
    pallas_call x1, Pallas kernels, shards(): pl.pallas_call(local_kernel, out_shape=(shape((owners, 2 * share + EXTRA,...  3.4 us
    all_gather x1, blocking collectives, shards(): x = lax.all_gather(exchange(copies, 'y', Y_ORDER), 'core', axis=0)  2.17 us

profile of v4, /device:TPU:8, one launch (start us, length us, event | category | flops | bytes accessed | tf_op | source)
XLA Modules:
  0.0 68.3 jit_solution(5800540728909668675)
XLA Ops:
  0.0 0.9 %broadcast_in_dim.2 = bf16[4,16,2048]{2,1,0:T(8,128)(2,1)S(1)} broadcast(bf16[16,2048]{1,0:T(8,128)(2,1)} %param.7), dimensions={1,2} | broadcast | bytes 327680 | tf_op jit(solution)/shard_map/broadcast_in_dim | solution.py:233
  0.9 13.1 %all_to_all.20 = bf16[4,16,2048]{2,1,0:T(8,128)(2,1)S(1)} all-to-all(bf16[4,16,2048]{2,1,0:T(8,128)(2,1)S(1)} %broadcast_in_dim.2), channel_id=1, replica_groups={{0,4,2,6},{7,3,5,1},{8,12,10,14},{15,11,13,9},{16,20,18,22},{23,19,21,1..., dimensions={0} | all-to-all | bytes 524288 | tf_op jit(solution)/shard_map/all_to_all | solution.py:39
  13.9 2.2 %all-gather = bf16[8,16,2048]{2,1,0:T(8,128)(2,1)S(1)} all-gather(bf16[4,16,2048]{2,1,0:T(8,128)(2,1)S(1)} %all_to_all.20), channel_id=2, replica_groups=mesh['zgroup'=8,'zpart'=2,'x'=4,'y'=4,'core'=2] {'core'}, dimensions={0}, use_global_device_ids=true | all-gather | bytes 786432 | tf_op jit(solution)/shard_map/all_gather | solution.py:234
  16.1 3.4 %shard_map.73 = (bf16[8,136,128]{2,1,0:T(8,128)(2,1)S(1)}, f32[128,512]{1,0:T(8,128)S(1)}, bf16[128,256]{1,0:T(8,128)(2,1)S(1)}, f32[128,16]{1,0:T(8,128)S(1)}) custom-call(bf16[2,4,16,2048]{3,2,1,0:T(8,128)(2,1)S(1)} %bitcast.2, bf16[2,8,2048]{2,1,0:T(8,128)(2,1)} %bitcast.3, f32[2,8]{1,0:T(2,128)} %refs_1_.1, f32[8]{0:T(128)} %refs_2_.1, f32[8]{0:T(128)} %refs_3_.1, ...), custom_call_target="tpu_custom_call" | custom-call | flops 700000000 | bytes 6291456 | tf_op jit(solution)/shard_map/pallas_call | solution.py:237
  19.5 10.7 %all_to_all.21.got_ref = bf16[8,136,128]{2,1,0:T(8,128)(2,1)S(1)} all-to-all(bf16[8,136,128]{2,1,0:T(8,128)(2,1)S(1)} %get-tuple-element.9), channel_id=1, replica_groups=mesh['zgroup'=8,'zpart'=2,'x'=4,'y'=4,'core'=2] {'zpart','x'}, dimensions={0} | all-to-all | bytes 557056 | tf_op jit(solution)/shard_map/all_to_all | solution.py:252
  30.2 0.1 shard_map.74
  30.3 26.0 %all_to_all.22.totals_ref = bf16[8,72,128]{2,1,0:T(8,128)(2,1)S(1)} all-to-all(bf16[8,72,128]{2,1,0:T(8,128)(2,1)S(1)} %shard_map.74), channel_id=1, replica_groups={{0,256,128,384,64,320,192,448},{449,193,321,65,385,129,257,1},{2,258,13..., dimensions={0} | all-to-all | bytes 294912 | tf_op jit(solution)/shard_map/all_to_all | solution.py:39
  56.3 0.1 shard_map.75
  56.4 10.9 %all_to_all.23.state_ref = bf16[8,128,128]{2,1,0:T(8,128)(2,1)S(1)} all-to-all(bf16[8,128,128]{2,1,0:T(8,128)(2,1)S(1)} %shard_map.75), channel_id=1, replica_groups=mesh['zgroup'=8,'zpart'=2,'x'=4,'y'=4,'core'=2] {'zpart','x'}, dimensions={0} | all-to-all | bytes 524288 | tf_op jit(solution)/shard_map/all_to_all | solution.py:256
  67.3 1.0 %shard_map.76 = bf16[128,512]{1,0:T(8,128)(2,1)} custom-call(bf16[8,128,128]{2,1,0:T(8,128)(2,1)S(1)} %all_to_all.23.state_ref, bf16[128,256]{1,0:T(8,128)(2,1)S(1)} %get-tuple-element.10.out_ref, f32[128,16]{1,0:T(8,128)S(1)} %get-tuple-element.11.reach_ref, f32[128,512]{1,0:T(8,128)S(1)} %get-tuple-element.12.y_ref), custom_call_target="tpu_custom_call" | custom-call | flops 40000000 | bytes 1048576 | tf_op jit(solution)/shard_map/pallas_call | solution.py:257

commit v5 on v4

--- a/solution.py
+++ b/solution.py
@@ -11,8 +11,8 @@
 EXTRA = 8
 CUTS = 1
 DEPTH = 2
-Y_ORDER = (0, 2, 1, 3)
-Z_ORDER = (0, 4, 2, 6, 1, 5, 3, 7)
+Y_ORDER = (1, 3, 0, 2)
+Z_ORDER = (3, 7, 1, 5, 2, 6, 0, 4)
 F32 = jnp.float32
 BF16 = jnp.bfloat16
 LAST = (((1,), (1,)), ((), ()))

time: 68.6 us -> 65.4 us (0.953)
  blocking collectives: 62.8 us -> 59.6 us
    all_to_all x2, blocking collectives: 39.1 us -> 37.1 us  [exchange(): lax.all_to_all(array, (axis, 'core'), 0, 0, tiled=True, axis_index_groups...]
    all_to_all x1, blocking collectives: 10.9 us -> 9.64 us  [shards(): state = lax.all_to_all(back, ('zpart', 'x'), 0, 0, tiled=True)]
where the time goes in v5:
time: 65.4 us; the launch traced here: 65.2 us
  blocking collectives  59.6 us (91%)
  Pallas kernels  4.67 us (7%)
  local copies, waits for them, and re-layouts  0.86 us (1%)
    all_to_all x2, blocking collectives, exchange(): lax.all_to_all(array, (axis, 'core'), 0, 0, tiled=True, axis_index_groups...  37.1 us
    all_to_all x1, blocking collectives, shards(): got = lax.all_to_all(send, ('zpart', 'x'), 0, 0, tiled=True)  10.7 us
    all_to_all x1, blocking collectives, shards(): state = lax.all_to_all(back, ('zpart', 'x'), 0, 0, tiled=True)  9.64 us
    pallas_call x1, Pallas kernels, shards(): pl.pallas_call(local_kernel, out_shape=(shape((owners, 2 * share + EXTRA,...  3.4 us
    all_gather x1, blocking collectives, shards(): x = lax.all_gather(exchange(copies, 'y', Y_ORDER), 'core', axis=0)  2.17 us

profile of v5, /device:TPU:8, one launch (start us, length us, event | category | flops | bytes accessed | tf_op | source)
XLA Modules:
  0.0 65.2 jit_solution(17079832702986934849)
XLA Ops:
  0.0 0.9 %broadcast_in_dim.2 = bf16[4,16,2048]{2,1,0:T(8,128)(2,1)S(1)} broadcast(bf16[16,2048]{1,0:T(8,128)(2,1)} %param.7), dimensions={1,2} | broadcast | bytes 327680 | tf_op jit(solution)/shard_map/broadcast_in_dim | solution.py:233
  0.9 13.2 %all_to_all.20 = bf16[4,16,2048]{2,1,0:T(8,128)(2,1)S(1)} all-to-all(bf16[4,16,2048]{2,1,0:T(8,128)(2,1)S(1)} %broadcast_in_dim.2), channel_id=1, replica_groups={{2,6,0,4},{5,1,7,3},{10,14,8,12},{13,9,15,11},{18,22,16,20},{21,17,23,1..., dimensions={0} | all-to-all | bytes 524288 | tf_op jit(solution)/shard_map/all_to_all | solution.py:39
  14.1 2.2 %all-gather = bf16[8,16,2048]{2,1,0:T(8,128)(2,1)S(1)} all-gather(bf16[4,16,2048]{2,1,0:T(8,128)(2,1)S(1)} %all_to_all.20), channel_id=2, replica_groups=mesh['zgroup'=8,'zpart'=2,'x'=4,'y'=4,'core'=2] {'core'}, dimensions={0}, use_global_device_ids=true | all-gather | bytes 786432 | tf_op jit(solution)/shard_map/all_gather | solution.py:234
  16.3 3.4 %shard_map.73 = (bf16[8,136,128]{2,1,0:T(8,128)(2,1)S(1)}, f32[128,512]{1,0:T(8,128)S(1)}, bf16[128,256]{1,0:T(8,128)(2,1)S(1)}, f32[128,16]{1,0:T(8,128)S(1)}) custom-call(bf16[2,4,16,2048]{3,2,1,0:T(8,128)(2,1)S(1)} %bitcast.2, bf16[2,8,2048]{2,1,0:T(8,128)(2,1)} %bitcast.3, f32[2,8]{1,0:T(2,128)} %refs_1_.1, f32[8]{0:T(128)} %refs_2_.1, f32[8]{0:T(128)} %refs_3_.1, ...), custom_call_target="tpu_custom_call" | custom-call | flops 700000000 | bytes 6291456 | tf_op jit(solution)/shard_map/pallas_call | solution.py:237
  19.7 10.7 %all_to_all.21.got_ref = bf16[8,136,128]{2,1,0:T(8,128)(2,1)S(1)} all-to-all(bf16[8,136,128]{2,1,0:T(8,128)(2,1)S(1)} %get-tuple-element.9), channel_id=1, replica_groups=mesh['zgroup'=8,'zpart'=2,'x'=4,'y'=4,'core'=2] {'zpart','x'}, dimensions={0} | all-to-all | bytes 557056 | tf_op jit(solution)/shard_map/all_to_all | solution.py:252
  30.4 0.1 shard_map.74
  30.4 23.9 %all_to_all.22.totals_ref = bf16[8,72,128]{2,1,0:T(8,128)(2,1)S(1)} all-to-all(bf16[8,72,128]{2,1,0:T(8,128)(2,1)S(1)} %shard_map.74), channel_id=1, replica_groups={{192,448,64,320,128,384,0,256},{257,1,385,129,321,65,449,193},{194,450,..., dimensions={0} | all-to-all | bytes 294912 | tf_op jit(solution)/shard_map/all_to_all | solution.py:39
  54.3 0.1 shard_map.75
  54.5 9.6 %all_to_all.23.state_ref = bf16[8,128,128]{2,1,0:T(8,128)(2,1)S(1)} all-to-all(bf16[8,128,128]{2,1,0:T(8,128)(2,1)S(1)} %shard_map.75), channel_id=1, replica_groups=mesh['zgroup'=8,'zpart'=2,'x'=4,'y'=4,'core'=2] {'zpart','x'}, dimensions={0} | all-to-all | bytes 524288 | tf_op jit(solution)/shard_map/all_to_all | solution.py:256
  64.1 1.0 %shard_map.76 = bf16[128,512]{1,0:T(8,128)(2,1)} custom-call(bf16[8,128,128]{2,1,0:T(8,128)(2,1)S(1)} %all_to_all.23.state_ref, bf16[128,256]{1,0:T(8,128)(2,1)S(1)} %get-tuple-element.10.out_ref, f32[128,16]{1,0:T(8,128)S(1)} %get-tuple-element.11.reach_ref, f32[128,512]{1,0:T(8,128)S(1)} %get-tuple-element.12.y_ref), custom_call_target="tpu_custom_call" | custom-call | flops 40000000 | bytes 1048576 | tf_op jit(solution)/shard_map/pallas_call | solution.py:257

commit v6 on v5

--- a/solution.py
+++ b/solution.py
@@ -11,6 +11,7 @@
 EXTRA = 8
 CUTS = 1
 DEPTH = 2
+L_ORDER = (2, 6, 1, 5, 3, 7, 0, 4)
 Y_ORDER = (1, 3, 0, 2)
 Z_ORDER = (3, 7, 1, 5, 2, 6, 0, 4)
 F32 = jnp.float32
@@ -34,9 +35,9 @@
     return jnp.where(lax.axis_index("core") == 0, order.index(place), len(order) - 1 - order.index(place))
 
 
-def exchange(array, axis, order):
+def exchange(array, axes, order):
     groups = [[2 * place for place in order], [2 * place + 1 for place in reversed(order)]]
-    return lax.all_to_all(array, (axis, "core"), 0, 0, tiled=True, axis_index_groups=groups)
+    return lax.all_to_all(array, (*axes, "core"), 0, 0, tiled=True, axis_index_groups=groups)
 
 
 def split(value, first):
@@ -126,7 +127,7 @@
         tailed.append(jnp.concatenate(both, axis=1).astype(BF16))
         marks = (split(decay[:, h : h + 1], 0) + split(decay[:, g : g + 1], 2)).astype(BF16)
         for part in range(h * parts, (h + 1) * parts):
-            send_ref[part, 2 * share :] = marks
+            send_ref[member(part, L_ORDER), 2 * share :] = marks
 
     ready(waits[5])
     inner = dot(x, wi_ref[...]).astype(BF16)
@@ -139,8 +140,9 @@
             piece = dot(both[:, HEADDIM * (h % 2) : HEADDIM * (h % 2 + 1)], tailed[h], FIRST).astype(BF16)
             for part in range(parts):
                 rows = slice(part * share, (part + 1) * share)
-                send_ref[h * parts + part, :share] = piece[rows, :STATE]
-                send_ref[h * parts + part, share : 2 * share] = piece[rows, STATE:]
+                place = member(h * parts + part, L_ORDER)
+                send_ref[place, :share] = piece[rows, :STATE]
+                send_ref[place, share : 2 * share] = piece[rows, STATE:]
         stacked = jnp.concatenate([jnp.where(left, both, zero), jnp.where(left, zero, both)], axis=0)
         gains = jnp.where(left, gain[:, 2 * pair : 2 * pair + 1], gain[:, 2 * pair + 1 : 2 * pair + 2])
         mixing = jnp.concatenate(weights[2 * pair : 2 * pair + 2], axis=1)
@@ -163,9 +165,9 @@
     decay_f = decay_b = jnp.ones((1, STATE), F32)
     state_f = state_b = jnp.zeros((share, STATE), F32)
     for block in range(blocks):
-        decay, piece = forward_part(got_ref[block], share)
+        decay, piece = forward_part(got_ref[member(block, L_ORDER)], share)
         decay_f, state_f = decay * decay_f, decay * state_f + piece
-        decay, piece = backward_part(got_ref[blocks - 1 - block], share)
+        decay, piece = backward_part(got_ref[member(blocks - 1 - block, L_ORDER)], share)
         decay_b, state_b = decay * decay_b, decay * state_b + piece
     marks_f, marks_b = split(decay_f, 0).astype(BF16), split(decay_b, 0).astype(BF16)
     state_f, state_b = state_f.astype(BF16), state_b.astype(BF16)
@@ -187,10 +189,11 @@
         rows = totals_ref[member(other, Z_ORDER)].astype(F32)
         state_b = jnp.where(other > place, joined(rows[share:], 0) * state_b + rows[:share], state_b)
     for block in range(blocks):
-        back_ref[block, :share] = state_f.astype(BF16)
-        decay, piece = forward_part(got_ref[block], share)
+        here = member(block, L_ORDER)
+        back_ref[here, :share] = state_f.astype(BF16)
+        decay, piece = forward_part(got_ref[here], share)
         state_f = decay * state_f + piece
-        other = blocks - 1 - block
+        other = member(blocks - 1 - block, L_ORDER)
         back_ref[other, share:] = state_b.astype(BF16)
         decay, piece = backward_part(got_ref[other], share)
         state_b = decay * state_b + piece
@@ -199,8 +202,9 @@
 def final_kernel(state_ref, out_ref, reach_ref, y_ref, mixed_ref):
     owners, rows, _ = state_ref.shape
     share, heads = rows // 2, reach_ref.shape[1] // 2
-    ahead = state_ref[:, :share].reshape(owners * share, STATE)
-    behind = state_ref[:, share:].reshape(owners * share, STATE)
+    places = [member(owner, L_ORDER) for owner in range(owners)]
+    ahead = jnp.concatenate([state_ref[place, :share] for place in places], axis=0)
+    behind = jnp.concatenate([state_ref[place, share:] for place in places], axis=0)
     far_f = dot(out_ref[:, :STATE], ahead, LAST)
     far_b = dot(out_ref[:, STATE:], behind, LAST)
     reach = reach_ref[...]
@@ -231,7 +235,7 @@
     share = width // owners
     shape = jax.ShapeDtypeStruct
     copies = jnp.broadcast_to(hidden_in[None], (lax.axis_size("y"), *hidden_in.shape))
-    x = lax.all_gather(exchange(copies, "y", Y_ORDER), "core", axis=0)
+    x = lax.all_gather(exchange(copies, ("y",), Y_ORDER), "core", axis=0)
     sources = (w_step.transpose(0, 2, 1), step_bias, decay_rate, skip_gain, w_inout, w_inner)
     sources = tuple(pltpu.with_memory_space_constraint(a, pltpu.HBM) for a in sources)
     send, near, outs, reach = pl.pallas_call(
@@ -249,11 +253,11 @@
         compiler_params=pltpu.CompilerParams(vmem_limit_bytes=24 * 1024 * 1024),
         cost_estimate=pl.CostEstimate(flops=700_000_000, bytes_accessed=6 << 20, transcendentals=0),
     )(x, *sources)
-    got = lax.all_to_all(send, ("zpart", "x"), 0, 0, tiled=True)
+    got = exchange(send, ("zpart", "x"), L_ORDER)
     totals = call(total_kernel, shape((groups, share + EXTRA, STATE), BF16), 1_000_000)(got)
-    totals = exchange(totals, "zgroup", Z_ORDER)
+    totals = exchange(totals, ("zgroup",), Z_ORDER)
     back = call(scan_kernel, shape((owners, 2 * share, STATE), BF16), 1_000_000)(totals, got)
-    state = lax.all_to_all(back, ("zpart", "x"), 0, 0, tiled=True)
+    state = exchange(back, ("zpart", "x"), L_ORDER)
     return call(final_kernel, shape((SPAN, width), BF16), 40_000_000)(state, outs, reach, near)
 
 

time: 65.4 us -> 64.8 us (level)
  the two profiles are of different devices: /device:TPU:8 before, /device:TPU:4 now
where the time goes in v6:
time: 64.8 us; the launch traced here: 64.6 us
  blocking collectives  59 us (91%)
  Pallas kernels  4.65 us (7%)
  local copies, waits for them, and re-layouts  0.86 us (1%)
    all_to_all x4, blocking collectives, exchange(): lax.all_to_all(array, (*axes, 'core'), 0, 0, tiled=True, axis_index_group...  56.9 us
    pallas_call x1, Pallas kernels, shards(): pl.pallas_call(local_kernel, out_shape=(shape((owners, 2 * share + EXTRA,...  3.4 us
    all_gather x1, blocking collectives, shards(): x = lax.all_gather(exchange(copies, ('y',), Y_ORDER), 'core', axis=0)  2.17 us

profile of v6, /device:TPU:4, one launch (start us, length us, event | category | flops | bytes accessed | tf_op | source)
XLA Modules:
  0.0 64.6 jit_solution(13230660256735658640)
XLA Ops:
  0.0 0.9 %broadcast_in_dim.2 = bf16[4,16,2048]{2,1,0:T(8,128)(2,1)S(1)} broadcast(bf16[16,2048]{1,0:T(8,128)(2,1)} %param.7), dimensions={1,2} | broadcast | bytes 327680 | tf_op jit(solution)/shard_map/broadcast_in_dim | solution.py:237
  0.9 10.4 %all_to_all.20 = bf16[4,16,2048]{2,1,0:T(8,128)(2,1)S(1)} all-to-all(bf16[4,16,2048]{2,1,0:T(8,128)(2,1)S(1)} %broadcast_in_dim.2), channel_id=1, replica_groups={{2,6,0,4},{5,1,7,3},{10,14,8,12},{13,9,15,11},{18,22,16,20},{21,17,23,1..., dimensions={0} | all-to-all | bytes 524288 | tf_op jit(solution)/shard_map/all_to_all | solution.py:40
  11.3 2.2 %all-gather = bf16[8,16,2048]{2,1,0:T(8,128)(2,1)S(1)} all-gather(bf16[4,16,2048]{2,1,0:T(8,128)(2,1)S(1)} %all_to_all.20), channel_id=2, replica_groups=mesh['zgroup'=8,'zpart'=2,'x'=4,'y'=4,'core'=2] {'core'}, dimensions={0}, use_global_device_ids=true | all-gather | bytes 786432 | tf_op jit(solution)/shard_map/all_gather | solution.py:238
  13.4 3.4 %shard_map.73 = (bf16[8,136,128]{2,1,0:T(8,128)(2,1)S(1)}, f32[128,512]{1,0:T(8,128)S(1)}, bf16[128,256]{1,0:T(8,128)(2,1)S(1)}, f32[128,16]{1,0:T(8,128)S(1)}) custom-call(bf16[2,4,16,2048]{3,2,1,0:T(8,128)(2,1)S(1)} %bitcast.2, bf16[2,8,2048]{2,1,0:T(8,128)(2,1)} %bitcast.3, f32[2,8]{1,0:T(2,128)} %refs_1_.1, f32[8]{0:T(128)} %refs_2_.1, f32[8]{0:T(128)} %refs_3_.1, ...), custom_call_target="tpu_custom_call" | custom-call | flops 700000000 | bytes 6291456 | tf_op jit(solution)/shard_map/pallas_call | solution.py:241
  16.8 12.8 %all_to_all.21.got_ref = bf16[8,136,128]{2,1,0:T(8,128)(2,1)S(1)} all-to-all(bf16[8,136,128]{2,1,0:T(8,128)(2,1)S(1)} %get-tuple-element.9), channel_id=1, replica_groups={{16,48,8,40,24,56,0,32},{33,1,57,25,41,9,49,17},{18,50,10,42,26,58,2,34..., dimensions={0} | all-to-all | bytes 557056 | tf_op jit(solution)/shard_map/all_to_all | solution.py:40
  29.6 0.1 shard_map.74
  29.7 23.3 %all_to_all.22.totals_ref = bf16[8,72,128]{2,1,0:T(8,128)(2,1)S(1)} all-to-all(bf16[8,72,128]{2,1,0:T(8,128)(2,1)S(1)} %shard_map.74), channel_id=1, replica_groups={{192,448,64,320,128,384,0,256},{257,1,385,129,321,65,449,193},{194,450,..., dimensions={0} | all-to-all | bytes 294912 | tf_op jit(solution)/shard_map/all_to_all | solution.py:40
  53.0 0.1 shard_map.75
  53.2 10.4 %all_to_all.23.state_ref = bf16[8,128,128]{2,1,0:T(8,128)(2,1)S(1)} all-to-all(bf16[8,128,128]{2,1,0:T(8,128)(2,1)S(1)} %shard_map.75), channel_id=1, replica_groups={{16,48,8,40,24,56,0,32},{33,1,57,25,41,9,49,17},{18,50,10,42,26,58,2,34..., dimensions={0} | all-to-all | bytes 524288 | tf_op jit(solution)/shard_map/all_to_all | solution.py:40
  63.5 1.0 %shard_map.76 = bf16[128,512]{1,0:T(8,128)(2,1)} custom-call(bf16[8,128,128]{2,1,0:T(8,128)(2,1)S(1)} %all_to_all.23.state_ref, bf16[128,256]{1,0:T(8,128)(2,1)S(1)} %get-tuple-element.10.out_ref, f32[128,16]{1,0:T(8,128)S(1)} %get-tuple-element.11.reach_ref, f32[128,512]{1,0:T(8,128)S(1)} %get-tuple-element.12.y_ref), custom_call_target="tpu_custom_call" | custom-call | flops 40000000 | bytes 1048576 | tf_op jit(solution)/shard_map/pallas_call | solution.py:261

commit v7 on v6

--- a/solution.py
+++ b/solution.py
@@ -11,8 +11,8 @@
 EXTRA = 8
 CUTS = 1
 DEPTH = 2
-L_ORDER = (2, 6, 1, 5, 3, 7, 0, 4)
-Y_ORDER = (1, 3, 0, 2)
+L_ORDER = (2, 6, 3, 7, 1, 5, 0, 4)
+Y_ORDER = (2, 0, 3, 1)
 Z_ORDER = (3, 7, 1, 5, 2, 6, 0, 4)
 F32 = jnp.float32
 BF16 = jnp.bfloat16

time: 64.8 us -> 64.5 us (level)
  no operation moved by 1% of the time
where the time goes in v7:
time: 64.5 us; the launch traced here: 64.3 us
  blocking collectives  58.7 us (91%)
  Pallas kernels  4.65 us (7%)
  local copies, waits for them, and re-layouts  0.86 us (1%)
    all_to_all x4, blocking collectives, exchange(): lax.all_to_all(array, (*axes, 'core'), 0, 0, tiled=True, axis_index_group...  56.6 us
    pallas_call x1, Pallas kernels, shards(): pl.pallas_call(local_kernel, out_shape=(shape((owners, 2 * share + EXTRA,...  3.4 us
    all_gather x1, blocking collectives, shards(): x = lax.all_gather(exchange(copies, ('y',), Y_ORDER), 'core', axis=0)  2.17 us

profile of v7, /device:TPU:4, one launch (start us, length us, event | category | flops | bytes accessed | tf_op | source)
XLA Modules:
  0.0 64.3 jit_solution(17032317758423410006)
XLA Ops:
  0.0 0.9 %broadcast_in_dim.2 = bf16[4,16,2048]{2,1,0:T(8,128)(2,1)S(1)} broadcast(bf16[16,2048]{1,0:T(8,128)(2,1)} %param.7), dimensions={1,2} | broadcast | bytes 327680 | tf_op jit(solution)/shard_map/broadcast_in_dim | solution.py:237
  0.9 10.1 %all_to_all.20 = bf16[4,16,2048]{2,1,0:T(8,128)(2,1)S(1)} all-to-all(bf16[4,16,2048]{2,1,0:T(8,128)(2,1)S(1)} %broadcast_in_dim.2), channel_id=1, replica_groups={{4,0,6,2},{3,7,1,5},{12,8,14,10},{11,15,9,13},{20,16,22,18},{19,23,17,2..., dimensions={0} | all-to-all | bytes 524288 | tf_op jit(solution)/shard_map/all_to_all | solution.py:40
  11.0 2.2 %all-gather = bf16[8,16,2048]{2,1,0:T(8,128)(2,1)S(1)} all-gather(bf16[4,16,2048]{2,1,0:T(8,128)(2,1)S(1)} %all_to_all.20), channel_id=2, replica_groups=mesh['zgroup'=8,'zpart'=2,'x'=4,'y'=4,'core'=2] {'core'}, dimensions={0}, use_global_device_ids=true | all-gather | bytes 786432 | tf_op jit(solution)/shard_map/all_gather | solution.py:238
  13.2 3.4 %shard_map.73 = (bf16[8,136,128]{2,1,0:T(8,128)(2,1)S(1)}, f32[128,512]{1,0:T(8,128)S(1)}, bf16[128,256]{1,0:T(8,128)(2,1)S(1)}, f32[128,16]{1,0:T(8,128)S(1)}) custom-call(bf16[2,4,16,2048]{3,2,1,0:T(8,128)(2,1)S(1)} %bitcast.2, bf16[2,8,2048]{2,1,0:T(8,128)(2,1)} %bitcast.3, f32[2,8]{1,0:T(2,128)} %refs_1_.1, f32[8]{0:T(128)} %refs_2_.1, f32[8]{0:T(128)} %refs_3_.1, ...), custom_call_target="tpu_custom_call" | custom-call | flops 700000000 | bytes 6291456 | tf_op jit(solution)/shard_map/pallas_call | solution.py:241
  16.6 12.4 %all_to_all.21.got_ref = bf16[8,136,128]{2,1,0:T(8,128)(2,1)S(1)} all-to-all(bf16[8,136,128]{2,1,0:T(8,128)(2,1)S(1)} %get-tuple-element.9), channel_id=1, replica_groups={{16,48,24,56,8,40,0,32},{33,1,41,9,57,25,49,17},{18,50,26,58,10,42,2,34..., dimensions={0} | all-to-all | bytes 557056 | tf_op jit(solution)/shard_map/all_to_all | solution.py:40
  29.0 0.1 shard_map.74
  29.1 23.7 %all_to_all.22.totals_ref = bf16[8,72,128]{2,1,0:T(8,128)(2,1)S(1)} all-to-all(bf16[8,72,128]{2,1,0:T(8,128)(2,1)S(1)} %shard_map.74), channel_id=1, replica_groups={{192,448,64,320,128,384,0,256},{257,1,385,129,321,65,449,193},{194,450,..., dimensions={0} | all-to-all | bytes 294912 | tf_op jit(solution)/shard_map/all_to_all | solution.py:40
  52.8 0.1 shard_map.75
  52.9 10.3 %all_to_all.23.state_ref = bf16[8,128,128]{2,1,0:T(8,128)(2,1)S(1)} all-to-all(bf16[8,128,128]{2,1,0:T(8,128)(2,1)S(1)} %shard_map.75), channel_id=1, replica_groups={{16,48,24,56,8,40,0,32},{33,1,41,9,57,25,49,17},{18,50,26,58,10,42,2,34..., dimensions={0} | all-to-all | bytes 524288 | tf_op jit(solution)/shard_map/all_to_all | solution.py:40
  63.2 1.0 %shard_map.76 = bf16[128,512]{1,0:T(8,128)(2,1)} custom-call(bf16[8,128,128]{2,1,0:T(8,128)(2,1)S(1)} %all_to_all.23.state_ref, bf16[128,256]{1,0:T(8,128)(2,1)S(1)} %get-tuple-element.10.out_ref, f32[128,16]{1,0:T(8,128)S(1)} %get-tuple-element.11.reach_ref, f32[128,512]{1,0:T(8,128)S(1)} %get-tuple-element.12.y_ref), custom_call_target="tpu_custom_call" | custom-call | flops 40000000 | bytes 1048576 | tf_op jit(solution)/shard_map/pallas_call | solution.py:261

commit v8 on v7

--- a/solution.py
+++ b/solution.py
@@ -12,7 +12,7 @@
 CUTS = 1
 DEPTH = 2
 L_ORDER = (2, 6, 3, 7, 1, 5, 0, 4)
-Y_ORDER = (2, 0, 3, 1)
+Y_ORDER = (1, 2, 0, 3)
 Z_ORDER = (3, 7, 1, 5, 2, 6, 0, 4)
 F32 = jnp.float32
 BF16 = jnp.bfloat16

time: 64.5 us -> 64.8 us (level)
  no operation moved by 1% of the time
where the time goes in v8:
time: 64.8 us; the launch traced here: 64.5 us
  blocking collectives  59 us (91%)
  Pallas kernels  4.64 us (7%)
  local copies, waits for them, and re-layouts  0.86 us (1%)
    all_to_all x4, blocking collectives, exchange(): lax.all_to_all(array, (*axes, 'core'), 0, 0, tiled=True, axis_index_group...  56.8 us
    pallas_call x1, Pallas kernels, shards(): pl.pallas_call(local_kernel, out_shape=(shape((owners, 2 * share + EXTRA,...  3.39 us
    all_gather x1, blocking collectives, shards(): x = lax.all_gather(exchange(copies, ('y',), Y_ORDER), 'core', axis=0)  2.17 us

profile of v8, /device:TPU:4, one launch (start us, length us, event | category | flops | bytes accessed | tf_op | source)
XLA Modules:
  0.0 64.5 jit_solution(14605561089440947496)
XLA Ops:
  0.0 0.9 %broadcast_in_dim.2 = bf16[4,16,2048]{2,1,0:T(8,128)(2,1)S(1)} broadcast(bf16[16,2048]{1,0:T(8,128)(2,1)} %param.7), dimensions={1,2} | broadcast | bytes 327680 | tf_op jit(solution)/shard_map/broadcast_in_dim | solution.py:237
  0.9 10.4 %all_to_all.20 = bf16[4,16,2048]{2,1,0:T(8,128)(2,1)S(1)} all-to-all(bf16[4,16,2048]{2,1,0:T(8,128)(2,1)S(1)} %broadcast_in_dim.2), channel_id=1, replica_groups={{2,4,0,6},{7,1,5,3},{10,12,8,14},{15,9,13,11},{18,20,16,22},{23,17,21,1..., dimensions={0} | all-to-all | bytes 524288 | tf_op jit(solution)/shard_map/all_to_all | solution.py:40
  11.3 2.2 %all-gather = bf16[8,16,2048]{2,1,0:T(8,128)(2,1)S(1)} all-gather(bf16[4,16,2048]{2,1,0:T(8,128)(2,1)S(1)} %all_to_all.20), channel_id=2, replica_groups=mesh['zgroup'=8,'zpart'=2,'x'=4,'y'=4,'core'=2] {'core'}, dimensions={0}, use_global_device_ids=true | all-gather | bytes 786432 | tf_op jit(solution)/shard_map/all_gather | solution.py:238
  13.4 3.4 %shard_map.73 = (bf16[8,136,128]{2,1,0:T(8,128)(2,1)S(1)}, f32[128,512]{1,0:T(8,128)S(1)}, bf16[128,256]{1,0:T(8,128)(2,1)S(1)}, f32[128,16]{1,0:T(8,128)S(1)}) custom-call(bf16[2,4,16,2048]{3,2,1,0:T(8,128)(2,1)S(1)} %bitcast.2, bf16[2,8,2048]{2,1,0:T(8,128)(2,1)} %bitcast.3, f32[2,8]{1,0:T(2,128)} %refs_1_.1, f32[8]{0:T(128)} %refs_2_.1, f32[8]{0:T(128)} %refs_3_.1, ...), custom_call_target="tpu_custom_call" | custom-call | flops 700000000 | bytes 6291456 | tf_op jit(solution)/shard_map/pallas_call | solution.py:241
  16.8 12.8 %all_to_all.21.got_ref = bf16[8,136,128]{2,1,0:T(8,128)(2,1)S(1)} all-to-all(bf16[8,136,128]{2,1,0:T(8,128)(2,1)S(1)} %get-tuple-element.9), channel_id=1, replica_groups={{16,48,24,56,8,40,0,32},{33,1,41,9,57,25,49,17},{18,50,26,58,10,42,2,34..., dimensions={0} | all-to-all | bytes 557056 | tf_op jit(solution)/shard_map/all_to_all | solution.py:40
  29.6 0.1 shard_map.74
  29.7 23.3 %all_to_all.22.totals_ref = bf16[8,72,128]{2,1,0:T(8,128)(2,1)S(1)} all-to-all(bf16[8,72,128]{2,1,0:T(8,128)(2,1)S(1)} %shard_map.74), channel_id=1, replica_groups={{192,448,64,320,128,384,0,256},{257,1,385,129,321,65,449,193},{194,450,..., dimensions={0} | all-to-all | bytes 294912 | tf_op jit(solution)/shard_map/all_to_all | solution.py:40
  53.0 0.1 shard_map.75
  53.2 10.3 %all_to_all.23.state_ref = bf16[8,128,128]{2,1,0:T(8,128)(2,1)S(1)} all-to-all(bf16[8,128,128]{2,1,0:T(8,128)(2,1)S(1)} %shard_map.75), channel_id=1, replica_groups={{16,48,24,56,8,40,0,32},{33,1,41,9,57,25,49,17},{18,50,26,58,10,42,2,34..., dimensions={0} | all-to-all | bytes 524288 | tf_op jit(solution)/shard_map/all_to_all | solution.py:40
  63.5 1.0 %shard_map.76 = bf16[128,512]{1,0:T(8,128)(2,1)} custom-call(bf16[8,128,128]{2,1,0:T(8,128)(2,1)S(1)} %all_to_all.23.state_ref, bf16[128,256]{1,0:T(8,128)(2,1)S(1)} %get-tuple-element.10.out_ref, f32[128,16]{1,0:T(8,128)S(1)} %get-tuple-element.11.reach_ref, f32[128,512]{1,0:T(8,128)S(1)} %get-tuple-element.12.y_ref), custom_call_target="tpu_custom_call" | custom-call | flops 40000000 | bytes 1048576 | tf_op jit(solution)/shard_map/pallas_call | solution.py:261
